TPU v7x, 512 devices: a whole 4x8x8 slice. The times are simulated.
512 devices in a mesh: prompt: 32 (over y, x), comp: 16 (over z, core).
Axes of the slice: x: 4, y: 8, z: 8, core: 2. Of those that a mesh axis runs over, the one named last changes fastest.
Arguments:
- queries: bfloat16 [16, 4096, 4096], P('comp', 'prompt')
- grad_out: bfloat16 [16, 4096, 4096], P('comp', 'prompt'), may hold values from -24 to 24
- outputs: bfloat16 [16, 4096, 4096], P('comp', 'prompt'), may hold values from -0.59765625 to 0.59765625
- completion_log_sum_exp: float32 [16, 32, 4096], P('comp', None, 'prompt'), may hold values from 7 to 11
- lengths: int32 [16], P('comp'), may hold values from 1 to 4096, 32768 in all
- shared_prompt_keys: bfloat16 [256, 512], P('prompt')
- shared_prompt_values: bfloat16 [256, 512], P('prompt'), may hold values from -0.5 to 0.5
Outputs:
- query_row_gradients: bfloat16 [16, 4096, 4096], P('comp', 'prompt')
- grad_prompt_keys: bfloat16 [256, 512], P('prompt')
- grad_prompt_values: bfloat16 [256, 512], P('prompt')
Inputs may be any that keep to these rules, and one draw needn't show every extreme that they name: `lengths`: one completion has length 4096.
All inputs are finite; a program needn't handle non-finite values. No bound on the sum of `lengths` on one device may be relied on, other than what follows from the above.
Results may differ from a plain program's by a relative error of at most 0.0054.
Values may be sent and summed in bfloat16 or wider, within the bound.
No kernel may reach another device: no remote copies, remote signals or barrier semaphores. Data moves between devices by JAX's collectives and lax.ppermute only.
A program may use at most 64 MiB of HBM per device.

v0:
```python
import jax
import jax.numpy as jnp
from jax import lax
from jax.sharding import PartitionSpec as P

HEAD_SIZE = 128


def head_group(q_part, g_part, o_part, rest, k_part, v_part, scale):
    scores = jnp.einsum("rhd,pd->hrp", q_part, k_part, preferred_element_type=jnp.float32) * scale
    total = jnp.logaddexp(rest, jax.nn.logsumexp(scores, axis=-1))
    probs = jnp.exp(scores - total[:, :, None])
    probs_low = probs.astype(jnp.bfloat16)
    delta = jnp.einsum("rhd,rhd->hr", g_part, o_part, preferred_element_type=jnp.float32)
    dprobs = jnp.einsum("rhd,pd->hrp", g_part, v_part, preferred_element_type=jnp.float32)
    dscores = (probs * (dprobs - delta[:, :, None])).astype(jnp.bfloat16)
    query_gradient = (
        jnp.einsum("hrp,pd->rhd", dscores, k_part, preferred_element_type=jnp.float32) * scale
    )
    key_gradient = (
        jnp.einsum("hrp,rhd->pd", dscores, q_part, preferred_element_type=jnp.float32) * scale
    )
    value_gradient = jnp.einsum(
        "hrp,rhd->pd", probs_low, g_part, preferred_element_type=jnp.float32
    )
    return (query_gradient, key_gradient, value_gradient)


def shards(
    queries,
    grad_out,
    outputs,
    completion_log_sum_exp,
    lengths,
    shared_prompt_keys,
    shared_prompt_values,
):
    keys_all, values_all = (
        lax.all_gather(shared_prompt_keys, "prompt", axis=0, tiled=True),
        lax.all_gather(shared_prompt_values, "prompt", axis=0, tiled=True),
    )
    rows = queries.shape[1]
    heads = completion_log_sum_exp.shape[1]
    kv_heads = shared_prompt_keys.shape[1] // HEAD_SIZE
    query_group = heads // kv_heads
    scale = 1.0 / HEAD_SIZE**0.5
    first_row = lax.axis_index("prompt") * rows
    live = first_row + jnp.arange(rows, dtype=jnp.int32) < lengths[0]
    masked_scores = grad_out[0] * live[:, None].astype(jnp.bfloat16)
    grad_parts = []
    key_parts = []
    value_parts = []
    for head_number in range(kv_heads):
        lo = head_number * query_group * HEAD_SIZE
        hi = lo + query_group * HEAD_SIZE
        q_part = queries[0][:, lo:hi].reshape(rows, query_group, HEAD_SIZE)
        g_part = masked_scores[:, lo:hi].reshape(rows, query_group, HEAD_SIZE)
        o_part = outputs[0][:, lo:hi].reshape(rows, query_group, HEAD_SIZE)
        rest = completion_log_sum_exp[
            0, head_number * query_group : (head_number + 1) * query_group
        ]
        k_part = keys_all[:, head_number * HEAD_SIZE : (head_number + 1) * HEAD_SIZE]
        v_part = values_all[:, head_number * HEAD_SIZE : (head_number + 1) * HEAD_SIZE]
        query_gradient, key_gradient, value_gradient = head_group(
            q_part, g_part, o_part, rest, k_part, v_part, scale
        )
        grad_parts.append(query_gradient.reshape(rows, query_group * HEAD_SIZE))
        key_parts.append(key_gradient)
        value_parts.append(value_gradient)
    grad_rows = jnp.concatenate(grad_parts, axis=1).astype(jnp.bfloat16)
    grad_rows, key_terms, value_terms = (
        grad_rows,
        jnp.concatenate(key_parts, axis=1),
        jnp.concatenate(value_parts, axis=1),
    )
    key_share, value_share = (
        lax.psum_scatter(key_terms, "prompt", scatter_dimension=0, tiled=True),
        lax.psum_scatter(value_terms, "prompt", scatter_dimension=0, tiled=True),
    )
    key_total, value_total = lax.psum((key_share, value_share), "comp")
    key_out = key_total.astype(jnp.bfloat16)
    value_out = value_total.astype(jnp.bfloat16)
    return (grad_rows[None], key_out, value_out)


def solution(mesh):
    in_specs = (
        P("comp", "prompt", None),
        P("comp", "prompt", None),
        P("comp", "prompt", None),
        P("comp", None, "prompt"),
        P("comp"),
        P("prompt", None),
        P("prompt", None),
    )
    out_specs = (P("comp", "prompt", None), P("prompt", None), P("prompt", None))
    return jax.shard_map(shards, mesh=mesh, in_specs=in_specs, out_specs=out_specs, check_vma=False)
```

profile of v0, /device:TPU:1, one launch (start us, length us, event | category | flops | bytes accessed | tf_op | source)
XLA Modules:
  0.0 633.4 jit_solution(11464396506221302994)
XLA Ops:
  7.9 38.7 %all_gather.6 = bf16[256,512]{1,0:T(8,128)(2,1)S(1)} all-gather(bf16[8,512]{1,0:T(8,128)(2,1)} %param.12), channel_id=1, replica_groups=mesh['prompt'=32,'comp'=16] {'prompt'}, dimensions={0}, use_global_device_ids=true | all-gather | bytes 270336 | tf_op jit(solution)/shard_map/all_gather | solution.py:39
  46.6 39.7 %all_gather.7 = bf16[256,512]{1,0:T(8,128)(2,1)} all-gather(bf16[8,512]{1,0:T(8,128)(2,1)} %param.13), channel_id=1, replica_groups=mesh['prompt'=32,'comp'=16] {'prompt'}, dimensions={0}, use_global_device_ids=true | all-gather | bytes 270336 | tf_op jit(solution)/shard_map/all_gather | solution.py:40
  86.2 1.6 copy.80
  87.9 0.8 fusion.44
  88.7 0.6 copy-done.26
  89.3 0.7 copy.82
  91.2 2.1 slice_bitcast_fusion.3
  93.7 1.0 copy.183
  95.3 0.3 copy-done.27
  96.0 0.3 fusion.48
  96.3 0.3 fusion.46
  96.6 0.6 copy-done.18
  97.2 1.1 fusion.49
  98.4 1.1 fusion.47
  99.6 0.3 exponential_reduce_fusion
  99.9 0.3 exponential_reduce_fusion.2
  100.2 0.4 copy-done.30
  100.9 0.3 fusion.15
  101.3 0.3 fusion.20
  101.6 0.3 copy-done.14
  101.9 0.3 fusion.14
  102.3 0.3 fusion.21
  102.6 0.3 copy-done.11
  102.9 0.3 fusion.12
  103.2 0.3 copy-done.20
  103.5 0.3 fusion.23
  103.9 0.3 fusion.13
  104.3 0.8 copy-done.6
  105.1 0.3 fusion.22
  105.5 0.8 pad_maximum_fusion.1
  106.3 2.0 copy.176
  108.4 1.4 convolution_bitcast_fusion.7
  109.9 0.3 convolution_bitcast_fusion.6
  110.2 0.6 copy-done.12
  110.8 0.3 convolution_bitcast_fusion.4
  111.1 0.3 convolution_bitcast_fusion.5
  111.5 1.0 copy.178
  113.0 0.3 fusion.17
  113.6 0.5 copy-done.5
  114.0 0.3 fusion.19
  114.9 1.0 pad_maximum_fusion
  116.0 231.9 %reduce-scatter.7.cloned.1.call-done = f32[8,512]{1,0:T(8,128)} async-done(((f32[256,512]{1,0:T(8,128)}), f32[8,512]{1,0:T(8,128)}) %reduce-scatter.7.cloned.1.call-update) | async-done | bytes 16400
  347.8 0.8 copy.177
  348.7 221.4 %reduce-scatter.9.cloned.1.call-done = f32[8,512]{1,0:T(8,128)} async-done(((f32[256,512]{1,0:T(8,128)}), f32[8,512]{1,0:T(8,128)}) %reduce-scatter.9.cloned.1.call-update) | async-done | bytes 16400
  570.1 0.8 copy.179
  570.9 54.3 %all-reduce = (bf16[8,512]{0,1:T(8,128)(2,1)S(1)}, bf16[8,512]{0,1:T(8,128)(2,1)S(1)}) all-reduce(f32[8,512]{0,1:T(8,128)S(1)} %copy.177, f32[8,512]{0,1:T(8,128)S(1)} %copy.179), channel_id=1, replica_groups=mesh['prompt'=32,'comp'=16] {'comp'}, use_global_device_ids=true, to_apply=%region_9.0 | all-reduce | flops 8192 | bytes 49152 | tf_op jit(solution)/shard_map/psum | solution.py:80
  625.2 0.7 copy.114
  625.9 0.7 copy.115
  (86 shorter events, 4.4 us)
Async XLA Ops:
  7.2 340.7 %reduce-scatter.7.cloned.1.call-start = ((), (), s32[]{:S(2)}) async-start(), calls=%async_computation.2 | async-start | bytes 540672
  46.6 49.7 %copy-start.24 = (bf16[256,512]{1,0:T(8,128)(2,1)}, bf16[256,512]{1,0:T(8,128)(2,1)S(1)}, u32[]{:S(2)}) copy-start(bf16[256,512]{1,0:T(8,128)(2,1)S(1)} %all_gather.6) | copy-start | bytes 786436
  87.9 1.4 copy-start.26
  89.3 6.7 %copy-start.19 = (bf16[128,1024]{0,1:T(8,128)(2,1)}, bf16[128,1024]{0,1:T(8,128)(2,1)S(1)}, u32[]{:S(2)}) copy-start(bf16[128,1024]{0,1:T(8,128)(2,1)S(1)} %get-tuple-element.19) | copy-start | bytes 786436
  89.3 7.0 %copy-start.22 = (bf16[128,1024]{0,1:T(8,128)(2,1)}, bf16[128,1024]{0,1:T(8,128)(2,1)S(1)}, u32[]{:S(2)}) copy-start(bf16[128,1024]{0,1:T(8,128)(2,1)S(1)} %get-tuple-element.18) | copy-start | bytes 786436
  90.1 0.7 copy-start.10
  90.1 0.8 copy-start.13
  90.1 0.9 copy-start.16
  93.6 1.4 copy-start.28
  94.7 1.0 copy-start.27
  96.3 1.0 copy-start.18
  96.6 1.8 copy-start.21
  99.5 2.1 copy-start
  99.9 0.8 copy-start.30
  99.9 1.0 copy-start.17
  99.9 1.1 copy-start.29
  100.2 1.1 copy-start.23
  100.9 1.0 copy-start.14
  101.3 1.0 copy-start.2
  101.9 0.9 copy-start.11
  102.2 0.9 copy-start.8
  102.6 1.0 copy-start.20
  103.5 0.8 copy-start.4
  104.3 0.8 copy-start.6
  108.4 461.7 %reduce-scatter.9.cloned.1.call-start = ((), (), s32[]{:S(2)}) async-start(), calls=%async_computation.3 | async-start | bytes 540672
  108.4 1.4 copy-start.1
  108.4 1.4 copy-start.15
  109.8 1.0 copy-start.12
  111.5 1.1 copy-start.3
  111.5 1.1 copy-start.25
  111.5 1.5 copy-start.9
  113.0 1.0 copy-start.5
  113.4 1.1 copy-start.7
Sparse Core Ops, SparseCore 0:
  108.5 239.2 reduce-scatter.6
  352.8 217.2 reduce-scatter.8
where the time goes:
time: 636 us; the launch traced here: 633 us
  waiting for transfers between devices  453 us (71%)
  blocking collectives  133 us (21%)
  local copies, waits for them, and re-layouts  19.8 us (3%)
  between operations  15.4 us (2%)
  matrix products  8.77 us (1%)
    unnamed x4, waiting for transfers between devices  453 us
    psum x1, blocking collectives, shards(): key_total, value_total = lax.psum((key_share, value_share), 'comp')  54.3 us
    all_gather x1, blocking collectives, shards(): lax.all_gather(shared_prompt_values, 'prompt', axis=0, tiled=True)  39.7 us
    all_gather x1, blocking collectives, shards(): lax.all_gather(shared_prompt_keys, 'prompt', axis=0, tiled=True)  38.7 us
    unnamed x79, local copies, waits for them, and re-layouts  18.1 us
  transfers between devices with their start and end apart: 2, of which 2 were waited for; matrix products, arithmetic and copies ran while one was open for 1% of the time, Pallas kernels for 0%

commit v1 on v0

v1 whole, which is shorter than its diff:
```python
import jax
import jax.numpy as jnp
from jax import lax
from jax.experimental import pallas as pl
from jax.experimental.pallas import tpu as pltpu
from jax.sharding import PartitionSpec as P

HEAD_SIZE = 128
LOG2_E = 1.4426950408889634


def rows_by_rows(a, b):
    return lax.dot_general(a, b, (((1,), (1,)), ((), ())), preferred_element_type=jnp.float32)


def columns_by_columns(a, b):
    return lax.dot_general(a, b, (((0,), (0,)), ((), ())), preferred_element_type=jnp.float32)


def attention_backward(live_ref, q_ref, g_ref, o_ref, rest_ref, k_ref, v_ref, dq_ref, dkv_ref):
    head = pl.program_id(0)
    rows = q_ref.shape[0]
    heads = q_ref.shape[1] // HEAD_SIZE
    kv_width = dkv_ref.shape[1] // 2
    scale = 1.0 / HEAD_SIZE**0.5
    live = lax.broadcasted_iota(jnp.int32, (rows, HEAD_SIZE), 0) < live_ref[0]
    keys = k_ref[...]
    values = v_ref[...]
    ones = jnp.ones((8, HEAD_SIZE), jnp.bfloat16)
    key_terms = jnp.zeros((keys.shape[0], HEAD_SIZE), jnp.float32)
    value_terms = jnp.zeros((keys.shape[0], HEAD_SIZE), jnp.float32)
    step = 2
    for first in range(0, heads, step):
        cut = [slice((first + i) * HEAD_SIZE, (first + i + 1) * HEAD_SIZE) for i in range(step)]
        q = jnp.concatenate([q_ref[:, c] for c in cut], axis=0)
        g = jnp.concatenate(
            [jnp.where(live, g_ref[:, c], jnp.zeros((), jnp.bfloat16)) for c in cut], axis=0
        )
        o = jnp.concatenate([o_ref[:, c] for c in cut], axis=0)
        rest = jnp.concatenate([rest_ref[first + i : first + i + 1, :] for i in range(step)], axis=1)
        rest = rest * LOG2_E
        scores = rows_by_rows(keys, q)
        top = jnp.maximum(jnp.max(scores, axis=0, keepdims=True) * (scale * LOG2_E), rest)
        weights = jnp.exp2(scores * (scale * LOG2_E) - top)
        total = jnp.sum(weights, axis=0, keepdims=True) + jnp.exp2(rest - top)
        probs = weights * (1.0 / total)
        product = g.astype(jnp.float32) * o.astype(jnp.float32)
        high = product.astype(jnp.bfloat16)
        low = (product - high.astype(jnp.float32)).astype(jnp.bfloat16)
        delta = (rows_by_rows(ones, high) + rows_by_rows(ones, low))[0:1]
        dprobs = rows_by_rows(values, g)
        dscores = (probs * (dprobs - delta)).astype(jnp.bfloat16)
        dq = (columns_by_columns(dscores, keys) * scale).astype(jnp.bfloat16)
        for i, c in enumerate(cut):
            dq_ref[:, c] = dq[i * rows : (i + 1) * rows]
        key_terms += jnp.dot(dscores, q, preferred_element_type=jnp.float32)
        value_terms += jnp.dot(
            probs.astype(jnp.bfloat16), g, preferred_element_type=jnp.float32
        )
    at = pl.multiple_of(head * HEAD_SIZE, HEAD_SIZE)
    dkv_ref[:, pl.ds(at, HEAD_SIZE)] = (key_terms * scale).astype(dkv_ref.dtype)
    dkv_ref[:, pl.ds(kv_width + at, HEAD_SIZE)] = value_terms.astype(dkv_ref.dtype)


def local_gradients(live, queries, grad_out, outputs, rest, kv):
    rows, width = queries.shape
    heads = rest.shape[0]
    prompt = kv.shape[0]
    kv_heads = kv.shape[1] // (2 * HEAD_SIZE)
    wide = width // kv_heads
    by_head = pl.BlockSpec((rows, wide), lambda h, live: (0, h))
    return pl.pallas_call(
        attention_backward,
        grid_spec=pltpu.PrefetchScalarGridSpec(
            num_scalar_prefetch=1,
            grid=(kv_heads,),
            in_specs=[
                by_head,
                by_head,
                by_head,
                pl.BlockSpec((heads // kv_heads, rows), lambda h, live: (h, 0)),
                pl.BlockSpec((prompt, HEAD_SIZE), lambda h, live: (0, h)),
                pl.BlockSpec((prompt, HEAD_SIZE), lambda h, live: (0, kv_heads + h)),
            ],
            out_specs=[by_head, pl.BlockSpec(kv.shape, lambda h, live: (0, 0))],
        ),
        out_shape=[
            jax.ShapeDtypeStruct(queries.shape, jnp.bfloat16),
            jax.ShapeDtypeStruct(kv.shape, jnp.bfloat16),
        ],
        compiler_params=pltpu.CompilerParams(
            dimension_semantics=("arbitrary",), vmem_limit_bytes=32 * 1024 * 1024
        ),
        name="attention_backward",
    )(live, queries, grad_out, outputs, rest, kv, kv)


def shards(
    queries,
    grad_out,
    outputs,
    completion_log_sum_exp,
    lengths,
    shared_prompt_keys,
    shared_prompt_values,
):
    rows = queries.shape[1]
    own, kv_width = shared_prompt_keys.shape
    owners = lax.axis_size("prompt")
    members = lax.axis_size("comp")
    kv_own = jnp.concatenate([shared_prompt_keys, shared_prompt_values], axis=1)
    kv_all = lax.all_to_all(
        jnp.broadcast_to(kv_own[None], (owners, own, 2 * kv_width)), "prompt", 0, 0
    )
    live = lengths - lax.axis_index("prompt") * rows
    grad_rows, terms = local_gradients(
        live,
        queries[0],
        grad_out[0],
        outputs[0],
        completion_log_sum_exp[0],
        kv_all.reshape(owners * own, 2 * kv_width),
    )
    shares = lax.all_to_all(terms.reshape(owners, own, 2 * kv_width), "prompt", 0, 0)
    share = jnp.sum(shares.astype(jnp.float32), axis=0).astype(jnp.bfloat16)
    parts = lax.all_to_all(
        jnp.broadcast_to(share[None], (members, own, 2 * kv_width)), "comp", 0, 0
    )
    total = jnp.sum(parts.astype(jnp.float32), axis=0).astype(jnp.bfloat16)
    return (grad_rows[None], total[:, :kv_width], total[:, kv_width:])


def solution(mesh):
    in_specs = (
        P("comp", "prompt", None),
        P("comp", "prompt", None),
        P("comp", "prompt", None),
        P("comp", None, "prompt"),
        P("comp"),
        P("prompt", None),
        P("prompt", None),
    )
    out_specs = (P("comp", "prompt", None), P("prompt", None), P("prompt", None))
    return jax.shard_map(shards, mesh=mesh, in_specs=in_specs, out_specs=out_specs, check_vma=False)
```

time: 636 us -> 87.6 us (0.14)
  waiting for transfers between devices: 453 us -> 15.6 us
  blocking collectives: 133 us -> 45.6 us
  local copies, waits for them, and re-layouts: 19.8 us -> 3.94 us
  between operations: 15.4 us -> 1.33 us
  starting transfers between devices: 0.08 us -> 10.5 us
  Pallas kernels: 0 us -> 9.26 us
  matrix products: 8.77 us -> 0 us
    unnamed x4 -> x0, waiting for transfers between devices: 453 us -> none
    all_gather x2 -> x0, blocking collectives: 78.4 us -> none  [the longest x1 39.7 us: shards(): lax.all_gather(shared_prompt_values, 'prompt', axis=0, tiled=True)]
    psum x1 -> x0, blocking collectives: 54.3 us -> none  [shards(): key_total, value_total = lax.psum((key_share, value_share), 'comp')]
    all_to_all x0 -> x2, blocking collectives: none -> 45.6 us  [the longest x1 25.6 us: shards(): lax.all_to_all(jnp.broadcast_to(share[None], (members, own, 2 * kv_width)...]
    unnamed x79 -> x8, local copies, waits for them, and re-layouts: 18.1 us -> 2.46 us
    all_to_all x0 -> x1, waiting for transfers between devices: none -> 15.6 us  [shards(): lax.all_to_all(jnp.broadcast_to(kv_own[None], (owners, own, 2 * kv_width)...]
    all_to_all x0 -> x1, starting transfers between devices: none -> 10.5 us  [shards(): lax.all_to_all(jnp.broadcast_to(kv_own[None], (owners, own, 2 * kv_width)...]
    pallas_call x0 -> x1, Pallas kernels: none -> 9.26 us  [local_gradients(): pl.pallas_call(attention_backward, grid_spec=pltpu.PrefetchScalarGridSpec...]
  transfers between devices with their start and end apart: 2 -> 1, of which waited for: 2 -> 1; matrix products, arithmetic and copies ran while one was open for 1% -> 0% of each run, Pallas kernels for 0% -> 0%
where the time goes in v1:
time: 87.6 us; the launch traced here: 87.2 us
  blocking collectives  45.6 us (52%)
  waiting for transfers between devices  15.6 us (18%)
  starting transfers between devices  10.5 us (12%)
  Pallas kernels  9.26 us (11%)
  local copies, waits for them, and re-layouts  3.94 us (4%)
  between operations  1.33 us (2%)
  other arithmetic  0.94 us (1%)
    all_to_all x1, blocking collectives, shards(): lax.all_to_all(jnp.broadcast_to(share[None], (members, own, 2 * kv_width)...  25.6 us
    all_to_all x1, blocking collectives, shards(): lax.all_to_all(terms.reshape(owners, own, 2 * kv_width), 'prompt', 0, 0)  20.1 us
    all_to_all x1, waiting for transfers between devices, shards(): lax.all_to_all(jnp.broadcast_to(kv_own[None], (owners, own, 2 * kv_width)...  15.6 us
    all_to_all x1, starting transfers between devices, shards(): lax.all_to_all(jnp.broadcast_to(kv_own[None], (owners, own, 2 * kv_width)...  10.5 us
    pallas_call x1, Pallas kernels, local_gradients(): pl.pallas_call(attention_backward, grid_spec=pltpu.PrefetchScalarGridSpec...  9.26 us
    unnamed x8, local copies, waits for them, and re-layouts  2.46 us
  transfers between devices with their start and end apart: 1, of which 1 were waited for; matrix products, arithmetic and copies ran while one was open for 0% of the time, Pallas kernels for 0%

profile of v1, /device:TPU:1, one launch (start us, length us, event | category | flops | bytes accessed | tf_op | source)
XLA Modules:
  0.0 87.2 jit_solution(10152871424371343830)
XLA Ops:
  0.6 0.0 copy-start
  0.6 0.8 pad_maximum_fusion
  1.4 0.9 broadcast_in_dim.6
  2.3 10.5 %all-to-all-start = ((bf16[32,8,1024]{2,1,0:T(8,128)(2,1)}), bf16[32,8,1024]{2,1,0:T(8,128)(2,1)S(1)}, u32[]{:S(2)}, u32[]{:S(2)}) async-start(bf16[32,8,1024]{2,1,0:T(8,128)(2,1)} %broadcast_in_dim.6), calls=%async_computation | async-start | bytes 1048576 | tf_op jit(solution)/shard_map/all_to_all | solution.py:112
  12.8 0.0 copy-start.3
  13.5 15.6 %all-to-all-done = bf16[32,8,1024]{2,1,0:T(8,128)(2,1)S(1)} async-done(((bf16[32,8,1024]{2,1,0:T(8,128)(2,1)}), bf16[32,8,1024]{2,1,0:T(8,128)(2,1)S(1)}, u32[]{:S(2)}, u32[]{:S(2)}) %all-to-all-start) | async-done | bytes 524320 | tf_op jit(solution)/shard_map/all_to_all | solution.py:112
  29.1 0.0 copy-done
  29.1 0.0 copy-done.3
  29.1 0.0 copy-start.1
  29.1 1.2 %copy-done.1 = bf16[1,128,4096]{2,1,0:T(8,128)(2,1)S(1)} copy-done((bf16[1,128,4096]{2,1,0:T(8,128)(2,1)S(1)}, bf16[1,128,4096]{2,1,0:T(8,128)(2,1)}, u32[]{:S(2)}) %copy-start.1) | copy-done | bytes 1048600
  30.3 0.0 copy-start.2
  30.3 1.2 %copy-done.2 = bf16[1,128,4096]{2,1,0:T(8,128)(2,1)S(1)} copy-done((bf16[1,128,4096]{2,1,0:T(8,128)(2,1)S(1)}, bf16[1,128,4096]{2,1,0:T(8,128)(2,1)}, u32[]{:S(2)}) %copy-start.2) | copy-done | bytes 1048600
  31.5 9.3 %attention_backward.1 = (bf16[128,4096]{1,0:T(8,128)(2,1)}, bf16[256,1024]{1,0:T(8,128)(2,1)S(1)}) custom-call(s32[1]{0:T(128)S(6)} %sub.7.live_ref, bf16[128,4096]{1,0:T(8,128)(2,1)S(1)} %bitcast.10, bf16[128,4096]{1,0:T(8,128)(2,1)S(1)} %bitcast.11, bf16[128,4096]{1,0:T(8,128)(2,1)S(1)} %bitcast.12, f32[32,128]{1,0:T(8,128)S(1)} %bitcast.14, ...), custom_call_target="tpu_custom_call" | custom-call | tf_op jit(solution)/shard_map/attention_backward/pallas_call | solution.py:72
  40.8 20.1 %all_to_all.15 = bf16[32,8,1024]{2,1,0:T(8,128)(2,1)S(1)} all-to-all(bf16[32,8,1024]{2,1,0:T(8,128)(2,1)S(1)} %bitcast.13), channel_id=1, replica_groups=mesh['prompt'=32,'comp'=16] {'prompt'}, dimensions={0} | all-to-all | bytes 1048576 | tf_op jit(solution)/shard_map/all_to_all | solution.py:124
  60.9 0.1 reduce_sum.24
  61.0 25.6 %all_to_all.16 = bf16[16,8,1024]{2,1,0:T(8,128)(2,1)S(1)} all-to-all(bf16[16,8,1024]{2,1,0:T(8,128)(2,1)S(1)} %broadcast_in_dim.8), channel_id=1, replica_groups=mesh['prompt'=32,'comp'=16] {'comp'}, dimensions={0} | all-to-all | bytes 524288 | tf_op jit(solution)/shard_map/all_to_all | solution.py:126
  86.6 0.6 fusion
  (2 shorter events, 0.1 us)
Async XLA Ops:
  0.6 28.5 %copy-start = (bf16[1,128,4096]{2,1,0:T(8,128)(2,1)S(1)}, bf16[1,128,4096]{2,1,0:T(8,128)(2,1)}, u32[]{:S(2)}) copy-start(bf16[1,128,4096]{2,1,0:T(8,128)(2,1)} %param.7) | copy-start | bytes 3145732
  2.3 26.8 %all-to-all-start = ((bf16[32,8,1024]{2,1,0:T(8,128)(2,1)}), bf16[32,8,1024]{2,1,0:T(8,128)(2,1)S(1)}, u32[]{:S(2)}, u32[]{:S(2)}) async-start(bf16[32,8,1024]{2,1,0:T(8,128)(2,1)} %broadcast_in_dim.6), calls=%async_computation | async-start | bytes 1048576 | tf_op jit(solution)/shard_map/all_to_all | solution.py:112
  12.8 16.3 %copy-start.3 = (f32[1,32,128]{2,1,0:T(8,128)S(1)}, f32[1,32,128]{2,1,0:T(8,128)}, u32[]{:S(2)}) copy-start(f32[1,32,128]{2,1,0:T(8,128)} %param.10) | copy-start | bytes 49156
  29.1 1.2 %copy-start.1 = (bf16[1,128,4096]{2,1,0:T(8,128)(2,1)S(1)}, bf16[1,128,4096]{2,1,0:T(8,128)(2,1)}, u32[]{:S(2)}) copy-start(bf16[1,128,4096]{2,1,0:T(8,128)(2,1)} %param.8) | copy-start | bytes 3145732
  30.3 1.2 %copy-start.2 = (bf16[1,128,4096]{2,1,0:T(8,128)(2,1)S(1)}, bf16[1,128,4096]{2,1,0:T(8,128)(2,1)}, u32[]{:S(2)}) copy-start(bf16[1,128,4096]{2,1,0:T(8,128)(2,1)} %param.9) | copy-start | bytes 3145732

commit v2 on v1

v2 whole, which is shorter than its diff:
```python
import functools

import jax
import jax.numpy as jnp
from jax import lax
from jax.experimental import pallas as pl
from jax.experimental.pallas import tpu as pltpu
from jax.sharding import PartitionSpec as P

HEAD_SIZE = 128
LOG2_E = 1.4426950408889634
CORES = 2
SMALL_VMEM = 8 * 1024 * 1024


def rows_by_rows(a, b):
    return lax.dot_general(a, b, (((1,), (1,)), ((), ())), preferred_element_type=jnp.float32)


def spread_kernel(core_ref, k_ref, v_ref, out_ref):
    half = k_ref.shape[1] // CORES
    at = pl.ds(pl.multiple_of(core_ref[0] * half, half), half)
    both = jnp.concatenate([k_ref[:, at], v_ref[:, at]], axis=1)
    for i in range(out_ref.shape[0]):
        out_ref[i] = both


def spread(core, keys, values, owners):
    own, width = keys.shape
    vmem = pl.BlockSpec(memory_space=pltpu.VMEM)
    return pl.pallas_call(
        spread_kernel,
        in_specs=[pl.BlockSpec(memory_space=pltpu.SMEM), vmem, vmem],
        out_specs=vmem,
        out_shape=jax.ShapeDtypeStruct((owners, own, 2 * width // CORES), keys.dtype),
        compiler_params=pltpu.CompilerParams(vmem_limit_bytes=SMALL_VMEM),
        name="spread",
    )(core, keys, values)


def delta_kernel(live_ref, g_ref, o_ref, delta_ref):
    rows, wide = o_ref.shape
    heads = wide // HEAD_SIZE
    step = pl.program_id(0)
    live = lax.broadcasted_iota(jnp.int32, (rows, HEAD_SIZE), 0) < live_ref[0]
    columns = []
    for h in range(heads):
        cut = slice(h * HEAD_SIZE, (h + 1) * HEAD_SIZE)
        at = pl.ds(pl.multiple_of(step * wide + h * HEAD_SIZE, HEAD_SIZE), HEAD_SIZE)
        product = g_ref[:, at].astype(jnp.float32) * o_ref[:, cut].astype(jnp.float32)
        columns.append(jnp.sum(jnp.where(live, product, 0.0), axis=1, keepdims=True))
    own = pl.ds(pl.multiple_of(step * heads, heads), heads)
    delta_ref[own, :] = jnp.concatenate(columns, axis=1).T


def row_delta(live, grad_out, outputs, heads, steps):
    rows, width = grad_out.shape
    vmem = pl.BlockSpec(memory_space=pltpu.VMEM)
    return pl.pallas_call(
        delta_kernel,
        grid=(steps,),
        in_specs=[
            pl.BlockSpec(memory_space=pltpu.SMEM),
            vmem,
            pl.BlockSpec((rows, width // steps), lambda h: (0, h)),
        ],
        out_specs=vmem,
        out_shape=jax.ShapeDtypeStruct((heads, rows), jnp.float32),
        cost_estimate=pl.CostEstimate(
            flops=3 * rows * width, bytes_accessed=4 * rows * width, transcendentals=0
        ),
        compiler_params=pltpu.CompilerParams(vmem_limit_bytes=SMALL_VMEM),
        name="delta",
    )(live, grad_out, outputs)


def backward_kernel(group, place_ref, q_ref, g_ref, rest_ref, delta_ref, kv_ref, *refs):
    dq_hbm, dkv_ref, dq_buf, out_sem = refs[-4:]
    steps, rows, wide = dq_buf.shape
    half = dkv_ref.shape[1] // 2
    scale = 1.0 / HEAD_SIZE**0.5
    first = place_ref[1] * steps
    live = lax.broadcasted_iota(jnp.int32, (rows, HEAD_SIZE), 0) < place_ref[0]
    stores = []
    for i in range(steps):
        keys = kv_ref[:, i * HEAD_SIZE : (i + 1) * HEAD_SIZE]
        values = kv_ref[:, half + i * HEAD_SIZE : half + (i + 1) * HEAD_SIZE]
        own = pl.ds(pl.multiple_of((first + i) * group, group), group)
        rest_rows = rest_ref[own, :] * LOG2_E
        delta_rows = delta_ref[own, :]
        rest = jnp.concatenate([rest_rows[h : h + 1] for h in range(group)], axis=1)
        delta = jnp.concatenate([delta_rows[h : h + 1] for h in range(group)], axis=1)
        at = pl.multiple_of((first + i) * wide, wide)
        columns = [pl.ds(at + h * HEAD_SIZE, HEAD_SIZE) for h in range(group)]
        q = jnp.concatenate([q_ref[:, cut] for cut in columns], axis=0)
        g = jnp.concatenate(
            [jnp.where(live, g_ref[:, cut], jnp.zeros((), jnp.bfloat16)) for cut in columns], axis=0
        )
        scores = rows_by_rows(keys, q)
        top = jnp.maximum(jnp.max(scores, axis=0, keepdims=True) * (scale * LOG2_E), rest)
        weights = jnp.exp2(scores * (scale * LOG2_E) - top)
        total = jnp.sum(weights, axis=0, keepdims=True) + jnp.exp2(rest - top)
        probs = weights * (1.0 / total)
        dprobs = rows_by_rows(values, g)
        dscores = (probs * (dprobs - delta)).astype(jnp.bfloat16)
        dq = jnp.dot(keys.T, dscores, preferred_element_type=jnp.float32) * scale
        dq = dq.astype(jnp.bfloat16)
        for h in range(group):
            dq_buf[i, :, h * HEAD_SIZE : (h + 1) * HEAD_SIZE] = dq[:, h * rows : (h + 1) * rows].T
        store = pltpu.make_async_copy(dq_buf.at[i], dq_hbm.at[:, pl.ds(at, wide)], out_sem.at[i])
        store.start()
        stores.append(store)
        key_terms = jnp.dot(dscores, q, preferred_element_type=jnp.float32) * scale
        value_terms = jnp.dot(probs.astype(jnp.bfloat16), g, preferred_element_type=jnp.float32)
        dkv_ref[:, i * HEAD_SIZE : (i + 1) * HEAD_SIZE] = key_terms.astype(dkv_ref.dtype)
        dkv_ref[:, half + i * HEAD_SIZE : half + (i + 1) * HEAD_SIZE] = value_terms.astype(
            dkv_ref.dtype
        )
    for store in stores:
        store.wait()


def half_gradients(place, queries, grad_out, rest, delta, kv, dtype, grad_rows=None):
    rows, width = queries.shape
    heads = rest.shape[0]
    prompt, columns = kv.shape
    steps = columns // (2 * HEAD_SIZE)
    wide = width // (CORES * steps)
    hbm = pl.BlockSpec(memory_space=pltpu.HBM)
    vmem = pl.BlockSpec(memory_space=pltpu.VMEM)
    operands = [place, queries, grad_out, rest, delta, kv]
    in_specs = [pl.BlockSpec(memory_space=pltpu.SMEM)] + [vmem] * 5
    aliases = {}
    if grad_rows is not None:
        operands.append(grad_rows)
        in_specs.append(hbm)
        aliases = {6: 0}
    products = rows * (heads // CORES) * prompt
    return pl.pallas_call(
        functools.partial(backward_kernel, wide // HEAD_SIZE),
        in_specs=in_specs,
        out_specs=[hbm, vmem],
        out_shape=[
            jax.ShapeDtypeStruct(queries.shape, queries.dtype),
            jax.ShapeDtypeStruct(kv.shape, dtype),
        ],
        scratch_shapes=[
            pltpu.VMEM((steps, rows, wide), queries.dtype),
            pltpu.SemaphoreType.DMA((steps,)),
        ],
        input_output_aliases=aliases,
        compiler_params=pltpu.CompilerParams(vmem_limit_bytes=40 * 1024 * 1024),
        cost_estimate=pl.CostEstimate(
            flops=10 * products * HEAD_SIZE, bytes_accessed=3 * rows * width, transcendentals=products
        ),
        name="attention_backward",
    )(*operands)


def finish_kernel(parts_ref, key_ref, value_ref):
    half = parts_ref.shape[2] // 2
    for core in range(CORES):
        total = parts_ref[core].astype(jnp.float32)
        for i in range(core + CORES, parts_ref.shape[0], CORES):
            total += parts_ref[i].astype(jnp.float32)
        at = slice((CORES - 1 - core) * half, (CORES - core) * half)
        key_ref[:, at] = total[:, :half].astype(key_ref.dtype)
        value_ref[:, at] = total[:, half:].astype(value_ref.dtype)


def finish(parts, like):
    return pl.pallas_call(
        finish_kernel,
        in_specs=[pl.BlockSpec(memory_space=pltpu.VMEM)],
        out_shape=[jax.ShapeDtypeStruct(like.shape, like.dtype)] * 2,
        compiler_params=pltpu.CompilerParams(vmem_limit_bytes=SMALL_VMEM),
        name="finish",
    )(parts)


def shards(
    queries,
    grad_out,
    outputs,
    completion_log_sum_exp,
    lengths,
    shared_prompt_keys,
    shared_prompt_values,
):
    rows = queries.shape[1]
    own, kv_width = shared_prompt_keys.shape
    heads = completion_log_sum_exp.shape[1]
    owners = lax.axis_size("prompt")
    members = lax.axis_size("comp")
    other_core = [(i, i ^ 1) for i in range(members)]
    core = lax.rem(lax.axis_index("comp"), CORES).astype(jnp.int32)
    live = lengths - lax.axis_index("prompt") * rows
    mine = jnp.concatenate([live, core[None]])
    others = jnp.concatenate([live, 1 - core[None]])
    rest = completion_log_sum_exp[0]

    near = lax.all_to_all(
        spread(core[None], shared_prompt_keys, shared_prompt_values, owners), "prompt", 0, 0
    ).reshape(owners * own, kv_width)
    delta = row_delta(live, grad_out[0], outputs[0], heads, kv_width // HEAD_SIZE)
    far = lax.ppermute(near, "comp", other_core)
    grad_rows, sent = half_gradients(
        mine, queries[0], grad_out[0], rest, delta, near, jnp.bfloat16
    )
    received = lax.ppermute(sent, "comp", other_core)
    grad_rows, kept = half_gradients(
        others, queries[0], grad_out[0], rest, delta, far, jnp.float32, grad_rows
    )
    terms = (kept + received.astype(jnp.float32)).astype(jnp.bfloat16)
    shares = lax.all_to_all(terms.reshape(owners, own, kv_width), "prompt", 0, 0)
    share = jnp.sum(shares.astype(jnp.float32), axis=0).astype(jnp.bfloat16)
    parts = lax.all_to_all(
        jnp.broadcast_to(share[None], (members, own, kv_width)), "comp", 0, 0
    )
    key_out, value_out = finish(parts, shared_prompt_keys)
    return (grad_rows[None], key_out, value_out)


def solution(mesh):
    in_specs = (
        P("comp", "prompt", None),
        P("comp", "prompt", None),
        P("comp", "prompt", None),
        P("comp", None, "prompt"),
        P("comp"),
        P("prompt", None),
        P("prompt", None),
    )
    out_specs = (P("comp", "prompt", None), P("prompt", None), P("prompt", None))
    return jax.shard_map(shards, mesh=mesh, in_specs=in_specs, out_specs=out_specs, check_vma=False)
```

time: 87.6 us -> 74.9 us (0.86)
  blocking collectives: 45.6 us -> 36.7 us
  waiting for transfers between devices: 15.6 us -> 6.9 us
  starting transfers between devices: 10.5 us -> 16.8 us
    all_to_all x2, blocking collectives: 45.6 us -> 36.7 us  [the longest x1 21.6 us: shards(): lax.all_to_all(jnp.broadcast_to(share[None], (members, own, kv_width)), '...]
    all_to_all x1, waiting for transfers between devices: 15.6 us -> 6.89 us  [shards(): lax.all_to_all(spread(core[None], shared_prompt_keys, shared_prompt_value...]
    ppermute x0 -> x2, starting transfers between devices: none -> 6.27 us  [the longest x1 4.35 us: shards(): far = lax.ppermute(near, 'comp', other_core)]
    unnamed x8 -> x14, local copies, waits for them, and re-layouts: 2.46 us -> 3.15 us
    pallas_call x1 -> x5, Pallas kernels: 9.26 us -> 9.23 us  [the longest x2 6.79 us: half_gradients(): pl.pallas_call(functools.partial(backward_kernel, wide // HEAD_SIZE), in_...]
  transfers between devices with their start and end apart: 1 -> 3, of which waited for: 1 -> 1; matrix products, arithmetic and copies ran while one was open for 0% -> 0% of each run, Pallas kernels for 0% -> 11%
where the time goes in v2:
time: 74.9 us; the launch traced here: 74.4 us
  blocking collectives  36.7 us (49%)
  starting transfers between devices  16.8 us (22%)
  Pallas kernels  9.23 us (12%)
  waiting for transfers between devices  6.9 us (9%)
  local copies, waits for them, and re-layouts  3.16 us (4%)
  between operations  1.4 us (2%)
    all_to_all x1, blocking collectives, shards(): lax.all_to_all(jnp.broadcast_to(share[None], (members, own, kv_width)), '...  21.6 us
    all_to_all x1, blocking collectives, shards(): lax.all_to_all(terms.reshape(owners, own, kv_width), 'prompt', 0, 0)  15.1 us
    all_to_all x1, starting transfers between devices, shards(): lax.all_to_all(spread(core[None], shared_prompt_keys, shared_prompt_value...  10.5 us
    all_to_all x1, waiting for transfers between devices, shards(): lax.all_to_all(spread(core[None], shared_prompt_keys, shared_prompt_value...  6.89 us
    pallas_call x2, Pallas kernels, half_gradients(): pl.pallas_call(functools.partial(backward_kernel, wide // HEAD_SIZE), in_...  6.79 us
    ppermute x1, starting transfers between devices, shards(): far = lax.ppermute(near, 'comp', other_core)  4.35 us
    unnamed x14, local copies, waits for them, and re-layouts  3.15 us
    ppermute x1, starting transfers between devices, shards(): received = lax.ppermute(sent, 'comp', other_core)  1.92 us
  transfers between devices with their start and end apart: 3, of which 1 were waited for; matrix products, arithmetic and copies ran while one was open for 0% of the time, Pallas kernels for 11%

profile of v2, /device:TPU:1, one launch (start us, length us, event | category | flops | bytes accessed | tf_op | source)
XLA Modules:
  0.0 74.4 jit_solution(2858382837146106274)
XLA Ops:
  0.6 0.0 copy-start.6
  0.6 0.0 copy-start.5
  0.7 0.7 copy-done.6
  1.3 0.0 copy-done.5
  1.3 0.7 spread.1
  2.1 10.5 %all-to-all-start = ((bf16[32,8,512]{2,1,0:T(8,128)(2,1)}), bf16[32,8,512]{2,1,0:T(8,128)(2,1)S(1)}, u32[]{:S(2)}, u32[]{:S(2)}) async-start(bf16[32,8,512]{2,1,0:T(8,128)(2,1)} %spread.1), calls=%async_computation | async-start | bytes 524288 | tf_op jit(solution)/shard_map/all_to_all | solution.py:202
  13.2 0.0 copy-start
  13.2 1.2 %copy-done = bf16[1,128,4096]{2,1,0:T(8,128)(2,1)S(1)} copy-done((bf16[1,128,4096]{2,1,0:T(8,128)(2,1)S(1)}, bf16[1,128,4096]{2,1,0:T(8,128)(2,1)}, u32[]{:S(2)}) %copy-start) | copy-done | bytes 1048600
  14.5 0.0 copy-start.2
  14.5 1.2 %copy-done.2 = bf16[1,128,4096]{2,1,0:T(8,128)(2,1)S(1)} copy-done((bf16[1,128,4096]{2,1,0:T(8,128)(2,1)S(1)}, bf16[1,128,4096]{2,1,0:T(8,128)(2,1)}, u32[]{:S(2)}) %copy-start.2) | copy-done | bytes 1048600
  15.7 0.0 copy-start.1
  15.7 0.0 copy-start.3
  15.7 0.0 copy-start.4
  15.7 1.1 %delta.1.delta_ref = f32[32,128]{1,0:T(8,128)S(1)} custom-call(s32[1]{0:T(128)S(6)} %sub.10.live_ref, bf16[128,4096]{1,0:T(8,128)(2,1)S(1)} %bitcast.10, bf16[128,4096]{1,0:T(8,128)(2,1)S(1)} %bitcast.13), custom_call_target="tpu_custom_call" | custom-call | flops 1572864 | bytes 2097152 | tf_op jit(solution)/shard_map/delta/pallas_call | solution.py:59
  16.8 0.1 pad_add_fusion.1.place_ref
  16.9 6.9 %all-to-all-done = bf16[32,8,512]{2,1,0:T(8,128)(2,1)S(1)} async-done(((bf16[32,8,512]{2,1,0:T(8,128)(2,1)}), bf16[32,8,512]{2,1,0:T(8,128)(2,1)S(1)}, u32[]{:S(2)}, u32[]{:S(2)}) %all-to-all-start) | async-done | bytes 262176 | tf_op jit(solution)/shard_map/all_to_all | solution.py:202
  23.8 4.3 %collective-permute-start = (bf16[256,512]{1,0:T(8,128)(2,1)S(1)}, bf16[256,512]{1,0:T(8,128)(2,1)S(1)}, u32[]{:S(2)}, u32[]{:S(2)}) collective-permute-start(bf16[256,512]{1,0:T(8,128)(2,1)S(1)} %bitcast.16), channel_id=1, source_target_pairs={{0,1},{1,0},{2,3},{3,2},{4,5},{5,4},{6,7},{7,6},{8,9},{9,8},{10,11... | collective-permute-start | bytes 786440 | tf_op jit(solution)/shard_map/ppermute | solution.py:206
  28.1 0.0 copy-done.1
  28.1 0.0 copy-done.3
  28.1 0.0 copy-done.4
  28.2 3.4 %attention_backward.2 = (bf16[128,4096]{1,0:T(8,128)(2,1)}, bf16[256,512]{1,0:T(8,128)(2,1)S(1)}) custom-call(s32[2]{0:T(128)S(1)} %pad_add_fusion.1.place_ref, bf16[128,4096]{1,0:T(8,128)(2,1)S(1)} %bitcast.14, bf16[128,4096]{1,0:T(8,128)(2,1)S(1)} %bitcast.11, f32[32,128]{1,0:T(8,128)S(1)} %bitcast.18, f32[32,128]{1,0:T(8,128)S(1)} %delta.1.delta_ref, ...), custom_call_target="tpu_custom_call" | custom-call | flops 671088640 | bytes 1572864 | tf_op jit(solution)/shard_map/attention_backward/pallas_call | solution.py:139
  31.5 1.9 %collective-permute-start.1 = (bf16[256,512]{1,0:T(8,128)(2,1)S(1)}, bf16[256,512]{1,0:T(8,128)(2,1)S(1)}, u32[]{:S(2)}, u32[]{:S(2)}) collective-permute-start(bf16[256,512]{1,0:T(8,128)(2,1)S(1)} %get-tuple-element.12), channel_id=1, source_target_pairs={{0,1},{1,0},{2,3},{3,2},{4,5},{5,4},{6,7},{7,6},{8,9},{9,8},{10,11... | collective-permute-start | bytes 786440 | tf_op jit(solution)/shard_map/ppermute | solution.py:210
  33.5 0.1 pad_add_fusion.place_ref
  33.5 0.0 collective-permute-done.kv_ref
  33.5 3.4 %attention_backward.3 = (bf16[128,4096]{1,0:T(8,128)(2,1)}, f32[256,512]{1,0:T(8,128)S(1)}) custom-call(s32[2]{0:T(128)S(1)} %pad_add_fusion.place_ref, bf16[128,4096]{1,0:T(8,128)(2,1)S(1)} %bitcast.15, bf16[128,4096]{1,0:T(8,128)(2,1)S(1)} %bitcast.12, f32[32,128]{1,0:T(8,128)S(1)} %bitcast.19, ...), custom_call_target="tpu_custom_call", output_to_operand_aliasing={{0}: (6, {})} | custom-call | flops 671088640 | bytes 1572864 | tf_op jit(solution)/shard_map/attention_backward/pallas_call | solution.py:139
  37.0 0.0 collective-permute-done.1
  37.0 0.1 fusion
  37.1 15.1 %all_to_all.15 = bf16[32,8,512]{2,1,0:T(8,128)(2,1)S(1)} all-to-all(bf16[32,8,512]{2,1,0:T(8,128)(2,1)S(1)} %fusion), channel_id=1, replica_groups=mesh['prompt'=32,'comp'=16] {'prompt'}, dimensions={0} | all-to-all | bytes 524288 | tf_op jit(solution)/shard_map/all_to_all | solution.py:215
  52.1 0.1 reduce_sum.12
  52.2 21.6 %all_to_all.16.parts_ref = bf16[16,8,512]{2,1,0:T(8,128)(2,1)S(1)} all-to-all(bf16[16,8,512]{2,1,0:T(8,128)(2,1)S(1)} %broadcast_in_dim.16), channel_id=1, replica_groups=mesh['prompt'=32,'comp'=16] {'comp'}, dimensions={0} | all-to-all | bytes 262144 | tf_op jit(solution)/shard_map/all_to_all | solution.py:217
  73.8 0.6 finish.1
  (1 shorter events, 0.0 us)
Async XLA Ops:
  0.6 0.7 copy-start.6
  0.6 0.7 copy-start.5
  2.1 21.7 %all-to-all-start = ((bf16[32,8,512]{2,1,0:T(8,128)(2,1)}), bf16[32,8,512]{2,1,0:T(8,128)(2,1)S(1)}, u32[]{:S(2)}, u32[]{:S(2)}) async-start(bf16[32,8,512]{2,1,0:T(8,128)(2,1)} %spread.1), calls=%async_computation | async-start | bytes 524288 | tf_op jit(solution)/shard_map/all_to_all | solution.py:202
  13.2 1.2 %copy-start = (bf16[1,128,4096]{2,1,0:T(8,128)(2,1)S(1)}, bf16[1,128,4096]{2,1,0:T(8,128)(2,1)}, u32[]{:S(2)}) copy-start(bf16[1,128,4096]{2,1,0:T(8,128)(2,1)} %param.8) | copy-start | bytes 3145732
  14.5 1.2 %copy-start.2 = (bf16[1,128,4096]{2,1,0:T(8,128)(2,1)S(1)}, bf16[1,128,4096]{2,1,0:T(8,128)(2,1)}, u32[]{:S(2)}) copy-start(bf16[1,128,4096]{2,1,0:T(8,128)(2,1)} %param.9) | copy-start | bytes 3145732
  15.7 12.4 %copy-start.1 = (bf16[1,128,4096]{2,1,0:T(8,128)(2,1)S(1)}, bf16[1,128,4096]{2,1,0:T(8,128)(2,1)}, u32[]{:S(2)}) copy-start(bf16[1,128,4096]{2,1,0:T(8,128)(2,1)} %param.8) | copy-start | bytes 3145732
  15.7 12.4 %copy-start.3 = (bf16[1,128,4096]{2,1,0:T(8,128)(2,1)S(1)}, bf16[1,128,4096]{2,1,0:T(8,128)(2,1)}, u32[]{:S(2)}) copy-start(bf16[1,128,4096]{2,1,0:T(8,128)(2,1)} %param.7) | copy-start | bytes 3145732
  15.7 12.5 %copy-start.4 = (f32[1,32,128]{2,1,0:T(8,128)S(1)}, f32[1,32,128]{2,1,0:T(8,128)}, u32[]{:S(2)}) copy-start(f32[1,32,128]{2,1,0:T(8,128)} %param.10) | copy-start | bytes 49156
  23.8 9.8 %collective-permute-start = (bf16[256,512]{1,0:T(8,128)(2,1)S(1)}, bf16[256,512]{1,0:T(8,128)(2,1)S(1)}, u32[]{:S(2)}, u32[]{:S(2)}) collective-permute-start(bf16[256,512]{1,0:T(8,128)(2,1)S(1)} %bitcast.16), channel_id=1, source_target_pairs={{0,1},{1,0},{2,3},{3,2},{4,5},{5,4},{6,7},{7,6},{8,9},{9,8},{10,11... | collective-permute-start | bytes 786440 | tf_op jit(solution)/shard_map/ppermute | solution.py:206
  31.5 5.4 %collective-permute-start.1 = (bf16[256,512]{1,0:T(8,128)(2,1)S(1)}, bf16[256,512]{1,0:T(8,128)(2,1)S(1)}, u32[]{:S(2)}, u32[]{:S(2)}) collective-permute-start(bf16[256,512]{1,0:T(8,128)(2,1)S(1)} %get-tuple-element.12), channel_id=1, source_target_pairs={{0,1},{1,0},{2,3},{3,2},{4,5},{5,4},{6,7},{7,6},{8,9},{9,8},{10,11... | collective-permute-start | bytes 786440 | tf_op jit(solution)/shard_map/ppermute | solution.py:210

commit v3 on v2

v3 whole, which is shorter than its diff:
```python
import functools

import jax
import jax.numpy as jnp
from jax import lax
from jax.experimental import pallas as pl
from jax.experimental.pallas import tpu as pltpu
from jax.sharding import PartitionSpec as P

HEAD_SIZE = 128
LOG2_E = 1.4426950408889634
CORES = 2
SMALL_VMEM = 8 * 1024 * 1024
LARGE_VMEM = 24 * 1024 * 1024
FULL_VMEM = 56 * 1024 * 1024
PIECES = 4


def rows_by_rows(a, b):
    return lax.dot_general(a, b, (((1,), (1,)), ((), ())), preferred_element_type=jnp.float32)


def own_core():
    return lax.rem(lax.axis_index("comp"), CORES)


def spread_kernel(k_hbm, v_hbm, out_hbm, half_buf, out_buf, in_sems, out_sems):
    half = half_buf.shape[2]
    at = pl.ds(pl.multiple_of(own_core() * half, half), half)
    loads = [
        pltpu.make_async_copy(ref.at[:, at], half_buf.at[i], in_sems.at[i])
        for i, ref in enumerate((k_hbm, v_hbm))
    ]
    for copy in loads:
        copy.start()
    for copy in loads:
        copy.wait()
    both = jnp.concatenate([half_buf[0], half_buf[1]], axis=1)
    pieces = out_sems.shape[0]
    piece = out_buf.shape[0] // pieces
    stores = []
    for i in range(pieces):
        for j in range(piece):
            out_buf[i * piece + j] = both
        own = pl.ds(i * piece, piece)
        stores.append(pltpu.make_async_copy(out_buf.at[own], out_hbm.at[own], out_sems.at[i]))
        stores[-1].start()
    for copy in stores:
        copy.wait()


def spread(keys, values, owners):
    own, width = keys.shape
    hbm = pl.BlockSpec(memory_space=pltpu.HBM)
    shape = (owners, own, 2 * width // CORES)
    return pl.pallas_call(
        spread_kernel,
        in_specs=[hbm, hbm],
        out_specs=hbm,
        out_shape=jax.ShapeDtypeStruct(shape, keys.dtype),
        scratch_shapes=[
            pltpu.VMEM((2, own, width // CORES), keys.dtype),
            pltpu.VMEM(shape, keys.dtype),
            pltpu.SemaphoreType.DMA((2,)),
            pltpu.SemaphoreType.DMA((4,)),
        ],
        compiler_params=pltpu.CompilerParams(vmem_limit_bytes=FULL_VMEM),
        name="spread",
    )(keys, values)


def delta_kernel(live_ref, g_ref, o_ref, delta_ref, keep_ref):
    rows, wide = o_ref.shape
    heads = wide // HEAD_SIZE
    step = pl.program_id(0)
    live = lax.broadcasted_iota(jnp.int32, (rows, HEAD_SIZE), 0) < live_ref[0]
    keep_ref[...] = live.astype(jnp.float32)
    columns = []
    for h in range(heads):
        cut = slice(h * HEAD_SIZE, (h + 1) * HEAD_SIZE)
        at = pl.ds(pl.multiple_of(step * wide + h * HEAD_SIZE, HEAD_SIZE), HEAD_SIZE)
        product = g_ref[:, at].astype(jnp.float32) * o_ref[:, cut].astype(jnp.float32)
        columns.append(jnp.sum(jnp.where(live, product, 0.0), axis=1, keepdims=True))
    own = pl.ds(pl.multiple_of(step * heads, heads), heads)
    delta_ref[own, :] = jnp.concatenate(columns, axis=1).T


def row_delta(live, grad_out, outputs, heads, steps):
    rows, width = grad_out.shape
    vmem = pl.BlockSpec(memory_space=pltpu.VMEM)
    return pl.pallas_call(
        delta_kernel,
        grid=(steps,),
        in_specs=[
            pl.BlockSpec(memory_space=pltpu.SMEM),
            vmem,
            pl.BlockSpec((rows, width // steps), lambda h: (0, h)),
        ],
        out_specs=[vmem, vmem],
        out_shape=[
            jax.ShapeDtypeStruct((heads, rows), jnp.float32),
            jax.ShapeDtypeStruct((rows, HEAD_SIZE), jnp.float32),
        ],
        compiler_params=pltpu.CompilerParams(vmem_limit_bytes=SMALL_VMEM),
        cost_estimate=pl.CostEstimate(
            flops=3 * rows * width, bytes_accessed=4 * rows * width, transcendentals=0
        ),
        name="delta",
    )(live, grad_out, outputs)


def scores_and_dprobs(keys, values, q, g):
    return rows_by_rows(keys, q), rows_by_rows(values, g)


def probs_and_dscores(scores, dprobs, rest, delta):
    scale = LOG2_E / HEAD_SIZE**0.5
    rest = rest * LOG2_E
    top = jnp.maximum(jnp.max(scores, axis=0, keepdims=True) * scale, rest)
    weights = jnp.exp2(scores * scale - top)
    total = jnp.sum(weights, axis=0, keepdims=True) + jnp.exp2(rest - top)
    probs = weights * (1.0 / total)
    dscores = probs * (dprobs - delta)
    return probs.astype(jnp.bfloat16), dscores.astype(jnp.bfloat16)


def side_by_side(tile):
    return jnp.concatenate([tile[h : h + 1] for h in range(tile.shape[0])], axis=1)


def place_half(side, half_ref, rows_hbm, sems):
    width = half_ref.shape[1]
    pieces = sems.shape[0]
    piece = width // pieces
    copies = []
    for i in range(pieces):
        to = pl.ds(pl.multiple_of(side * width + i * piece, piece), piece)
        copies.append(
            pltpu.make_async_copy(
                half_ref.at[:, i * piece : (i + 1) * piece], rows_hbm.at[:, to], sems.at[i]
            )
        )
        copies[-1].start()
    return copies


def backward_kernel(turn, q_ref, g_ref, rest_ref, delta_ref, keep_ref, kv_ref, *refs):
    if turn == 0:
        dq_ref, dkv_ref = refs
    else:
        before_ref, dq_ref, dkv_ref, rows_hbm, sems = refs
    rows, width = dq_ref.shape
    half = dkv_ref.shape[1] // 2
    steps = half // HEAD_SIZE
    wide = width // steps
    group = wide // HEAD_SIZE
    scale = 1.0 / HEAD_SIZE**0.5
    side = own_core() if turn == 0 else 1 - own_core()
    first = side * steps
    copies = []
    if turn == 1:
        copies = place_half(own_core(), before_ref, rows_hbm, sems)
    keep = keep_ref[...]
    q, g, p, ds, held = {}, {}, {}, {}, {}
    for i in range(steps):
        at = pl.multiple_of((first + i) * wide, wide)
        columns = [pl.ds(at + h * HEAD_SIZE, HEAD_SIZE) for h in range(group)]
        q[i] = jnp.concatenate([q_ref[:, cut] for cut in columns], axis=0)
        g[i] = jnp.concatenate(
            [(g_ref[:, cut].astype(jnp.float32) * keep).astype(jnp.bfloat16) for cut in columns],
            axis=0,
        )
        key_at = slice(i * HEAD_SIZE, (i + 1) * HEAD_SIZE)
        value_at = slice(half + i * HEAD_SIZE, half + (i + 1) * HEAD_SIZE)
        held[i] = scores_and_dprobs(kv_ref[:, key_at], kv_ref[:, value_at], q[i], g[i])
    for i in range(steps):
        own = pl.ds(pl.multiple_of((first + i) * group, group), group)
        p[i], ds[i] = probs_and_dscores(
            *held[i], side_by_side(rest_ref[own, :]), side_by_side(delta_ref[own, :])
        )
        keys = kv_ref[:, i * HEAD_SIZE : (i + 1) * HEAD_SIZE]
        dq = jnp.dot(keys.T, ds[i], preferred_element_type=jnp.float32) * scale
        dq = dq.astype(jnp.bfloat16)
        for h in range(group):
            cut = slice(i * wide + h * HEAD_SIZE, i * wide + (h + 1) * HEAD_SIZE)
            dq_ref[:, cut] = dq[:, h * rows : (h + 1) * rows].T
    for i in range(steps):
        key_terms = jnp.dot(ds[i], q[i], preferred_element_type=jnp.float32) * scale
        value_terms = jnp.dot(p[i], g[i], preferred_element_type=jnp.float32)
        dkv_ref[:, i * HEAD_SIZE : (i + 1) * HEAD_SIZE] = key_terms.astype(dkv_ref.dtype)
        dkv_ref[:, half + i * HEAD_SIZE : half + (i + 1) * HEAD_SIZE] = value_terms.astype(
            dkv_ref.dtype
        )
    for copy in copies:
        copy.wait()


def half_gradients(turn, queries, grad_out, rest, delta, keep, kv, *before):
    rows, width = queries.shape
    products = rows * (rest.shape[0] // CORES) * kv.shape[0]
    vmem = pl.BlockSpec(memory_space=pltpu.VMEM)
    out_specs = [vmem, vmem]
    out_shape = [
        jax.ShapeDtypeStruct((rows, width // CORES), queries.dtype),
        jax.ShapeDtypeStruct(kv.shape, jnp.float32 if turn else jnp.bfloat16),
    ]
    scratch = []
    if turn == 1:
        out_specs.append(pl.BlockSpec(memory_space=pltpu.HBM))
        out_shape.append(jax.ShapeDtypeStruct(queries.shape, queries.dtype))
        scratch.append(pltpu.SemaphoreType.DMA((PIECES,)))
    return pl.pallas_call(
        functools.partial(backward_kernel, turn),
        in_specs=[vmem] * (6 + len(before)),
        out_specs=out_specs,
        out_shape=out_shape,
        scratch_shapes=scratch,
        compiler_params=pltpu.CompilerParams(vmem_limit_bytes=LARGE_VMEM),
        cost_estimate=pl.CostEstimate(
            flops=10 * products * HEAD_SIZE, bytes_accessed=3 * rows * width, transcendentals=products
        ),
        name="attention_backward",
    )(queries, grad_out, rest, delta, keep, kv, *before)


def finish_kernel(
    parts_ref, far_ref, before_hbm, key_hbm, value_hbm, rows_hbm, key_buf, value_buf, sems, out_sems
):
    copies = place_half(1 - own_core(), far_ref, rows_hbm, sems)
    half = parts_ref.shape[2] // 2
    for core in range(CORES):
        total = parts_ref[core].astype(jnp.float32)
        for i in range(core + CORES, parts_ref.shape[0], CORES):
            total += parts_ref[i].astype(jnp.float32)
        at = slice((CORES - 1 - core) * half, (CORES - core) * half)
        key_buf[:, at] = total[:, :half].astype(key_buf.dtype)
        value_buf[:, at] = total[:, half:].astype(value_buf.dtype)
    for i, (buf, hbm) in enumerate(((key_buf, key_hbm), (value_buf, value_hbm))):
        copies.append(pltpu.make_async_copy(buf, hbm, out_sems.at[i]))
        copies[-1].start()
    for copy in copies:
        copy.wait()


def finish(parts, far, grad_rows, like):
    vmem = pl.BlockSpec(memory_space=pltpu.VMEM)
    hbm = pl.BlockSpec(memory_space=pltpu.HBM)
    one = jax.ShapeDtypeStruct(like.shape, like.dtype)
    return pl.pallas_call(
        finish_kernel,
        in_specs=[vmem, vmem, hbm],
        out_specs=[hbm, hbm, hbm],
        out_shape=[one, one, jax.ShapeDtypeStruct(grad_rows.shape, grad_rows.dtype)],
        scratch_shapes=[
            pltpu.VMEM(like.shape, like.dtype),
            pltpu.VMEM(like.shape, like.dtype),
            pltpu.SemaphoreType.DMA((PIECES,)),
            pltpu.SemaphoreType.DMA((2,)),
        ],
        input_output_aliases={2: 2},
        compiler_params=pltpu.CompilerParams(vmem_limit_bytes=SMALL_VMEM),
        name="finish",
    )(parts, far, grad_rows)


def shards(
    queries,
    grad_out,
    outputs,
    completion_log_sum_exp,
    lengths,
    shared_prompt_keys,
    shared_prompt_values,
):
    rows = queries.shape[1]
    own, kv_width = shared_prompt_keys.shape
    heads = completion_log_sum_exp.shape[1]
    owners = lax.axis_size("prompt")
    members = lax.axis_size("comp")
    other_core = [(i, i ^ 1) for i in range(members)]
    live = lengths - lax.axis_index("prompt") * rows
    rest = completion_log_sum_exp[0]

    near = lax.all_to_all(
        spread(shared_prompt_keys, shared_prompt_values, owners), "prompt", 0, 0
    ).reshape(owners * own, kv_width)
    delta, keep = row_delta(live, grad_out[0], outputs[0], heads, kv_width // HEAD_SIZE)
    far = lax.ppermute(near, "comp", other_core)
    grad_near, sent = half_gradients(0, queries[0], grad_out[0], rest, delta, keep, near)
    received = lax.ppermute(sent, "comp", other_core)
    grad_far, kept, grad_rows = half_gradients(
        1, queries[0], grad_out[0], rest, delta, keep, far, grad_near
    )
    terms = (kept + received.astype(jnp.float32)).astype(jnp.bfloat16)
    shares = lax.all_to_all(terms.reshape(owners, own, kv_width), "prompt", 0, 0)
    share = jnp.sum(shares.astype(jnp.float32), axis=0).astype(jnp.bfloat16)
    parts = lax.all_to_all(
        jnp.broadcast_to(share[None], (members, own, kv_width)), "comp", 0, 0
    )
    key_out, value_out, grad_rows = finish(parts, grad_far, grad_rows, shared_prompt_keys)
    return (grad_rows[None], key_out, value_out)


def solution(mesh):
    in_specs = (
        P("comp", "prompt", None),
        P("comp", "prompt", None),
        P("comp", "prompt", None),
        P("comp", None, "prompt"),
        P("comp"),
        P("prompt", None),
        P("prompt", None),
    )
    out_specs = (P("comp", "prompt", None), P("prompt", None), P("prompt", None))
    return jax.shard_map(shards, mesh=mesh, in_specs=in_specs, out_specs=out_specs, check_vma=False)
```

time: 74.9 us -> 72.6 us (0.969)
  Pallas kernels: 9.23 us -> 7.77 us
    pallas_call x4, Pallas kernels: 8.13 us -> 6.64 us  [the longest x2 4.32 us: half_gradients(): pl.pallas_call(functools.partial(backward_kernel, turn), in_specs=[vmem]...]
    unnamed x14 -> x10, local copies, waits for them, and re-layouts: 3.15 us -> 2.46 us
  transfers between devices with their start and end apart: 3 -> 3, of which waited for: 1 -> 1; matrix products, arithmetic and copies ran while one was open for 0% -> 0% of each run, Pallas kernels for 11% -> 8%
where the time goes in v3:
time: 72.6 us; the launch traced here: 72.2 us
  blocking collectives  36.7 us (51%)
  starting transfers between devices  16.8 us (23%)
  Pallas kernels  7.77 us (11%)
  waiting for transfers between devices  6.96 us (10%)
  local copies, waits for them, and re-layouts  2.47 us (3%)
  between operations  1.4 us (2%)
    all_to_all x1, blocking collectives, shards(): lax.all_to_all(jnp.broadcast_to(share[None], (members, own, kv_width)), '...  21.6 us
    all_to_all x1, blocking collectives, shards(): lax.all_to_all(terms.reshape(owners, own, kv_width), 'prompt', 0, 0)  15.1 us
    all_to_all x1, starting transfers between devices, shards(): lax.all_to_all(spread(shared_prompt_keys, shared_prompt_values, owners),...  10.5 us
    all_to_all x1, waiting for transfers between devices, shards(): lax.all_to_all(spread(shared_prompt_keys, shared_prompt_values, owners),...  6.95 us
    ppermute x1, starting transfers between devices, shards(): far = lax.ppermute(near, 'comp', other_core)  4.35 us
    pallas_call x2, Pallas kernels, half_gradients(): pl.pallas_call(functools.partial(backward_kernel, turn), in_specs=[vmem]...  4.32 us
    unnamed x10, local copies, waits for them, and re-layouts  2.46 us
    ppermute x1, starting transfers between devices, shards(): received = lax.ppermute(sent, 'comp', other_core)  1.92 us
  transfers between devices with their start and end apart: 3, of which 1 were waited for; matrix products, arithmetic and copies ran while one was open for 0% of the time, Pallas kernels for 8%

profile of v3, /device:TPU:1, one launch (start us, length us, event | category | flops | bytes accessed | tf_op | source)
XLA Modules:
  0.0 72.2 jit_solution(9308373467125983673)
XLA Ops:
  0.6 1.5 %spread.1 = bf16[32,8,512]{2,1,0:T(8,128)(2,1)} custom-call(bf16[8,512]{1,0:T(8,128)(2,1)} %k_hbm.1, bf16[8,512]{1,0:T(8,128)(2,1)} %v_hbm.1), custom_call_target="tpu_custom_call" | custom-call | tf_op jit(solution)/shard_map/spread/pallas_call | solution.py:56
  2.1 0.0 copy-start.4
  2.1 10.5 %all-to-all-start = ((bf16[32,8,512]{2,1,0:T(8,128)(2,1)}), bf16[32,8,512]{2,1,0:T(8,128)(2,1)S(1)}, u32[]{:S(2)}, u32[]{:S(2)}) async-start(bf16[32,8,512]{2,1,0:T(8,128)(2,1)} %spread.1), calls=%async_computation | async-start | bytes 524288 | tf_op jit(solution)/shard_map/all_to_all | solution.py:284
  13.3 0.0 copy-start
  13.3 1.2 %copy-done = bf16[1,128,4096]{2,1,0:T(8,128)(2,1)S(1)} copy-done((bf16[1,128,4096]{2,1,0:T(8,128)(2,1)S(1)}, bf16[1,128,4096]{2,1,0:T(8,128)(2,1)}, u32[]{:S(2)}) %copy-start) | copy-done | bytes 1048600
  14.5 0.0 copy-start.3
  14.5 1.2 %copy-done.3 = bf16[1,128,4096]{2,1,0:T(8,128)(2,1)S(1)} copy-done((bf16[1,128,4096]{2,1,0:T(8,128)(2,1)S(1)}, bf16[1,128,4096]{2,1,0:T(8,128)(2,1)}, u32[]{:S(2)}) %copy-start.3) | copy-done | bytes 1048600
  15.7 0.0 copy-start.1
  15.7 0.0 copy-start.2
  15.7 1.1 %delta.1 = (f32[32,128]{1,0:T(8,128)S(1)}, f32[128,128]{1,0:T(8,128)S(1)}) custom-call(s32[1]{0:T(128)S(6)} %sub.7.live_ref, bf16[128,4096]{1,0:T(8,128)(2,1)S(1)} %bitcast.9, bf16[128,4096]{1,0:T(8,128)(2,1)S(1)} %bitcast.14), custom_call_target="tpu_custom_call" | custom-call | flops 1572864 | bytes 2097152 | tf_op jit(solution)/shard_map/delta/pallas_call | solution.py:91
  16.9 7.0 %all-to-all-done = bf16[32,8,512]{2,1,0:T(8,128)(2,1)S(1)} async-done(((bf16[32,8,512]{2,1,0:T(8,128)(2,1)}), bf16[32,8,512]{2,1,0:T(8,128)(2,1)S(1)}, u32[]{:S(2)}, u32[]{:S(2)}) %all-to-all-start) | async-done | bytes 262176 | tf_op jit(solution)/shard_map/all_to_all | solution.py:284
  23.8 4.3 %collective-permute-start = (bf16[256,512]{1,0:T(8,128)(2,1)S(1)}, bf16[256,512]{1,0:T(8,128)(2,1)S(1)}, u32[]{:S(2)}, u32[]{:S(2)}) collective-permute-start(bf16[256,512]{1,0:T(8,128)(2,1)S(1)} %bitcast.15), channel_id=1, source_target_pairs={{0,1},{1,0},{2,3},{3,2},{4,5},{5,4},{6,7},{7,6},{8,9},{9,8},{10,11... | collective-permute-start | bytes 786440 | tf_op jit(solution)/shard_map/ppermute | solution.py:288
  28.2 0.0 copy-done.4
  28.2 0.0 copy-done.1
  28.2 0.0 copy-done.2
  28.2 2.1 %attention_backward.2 = (bf16[128,2048]{1,0:T(8,128)(2,1)S(1)}, bf16[256,512]{1,0:T(8,128)(2,1)S(1)}) custom-call(bf16[128,4096]{1,0:T(8,128)(2,1)S(1)} %bitcast.12, bf16[128,4096]{1,0:T(8,128)(2,1)S(1)} %bitcast.10, f32[32,128]{1,0:T(8,128)S(1)} %bitcast.17, f32[32,128]{1,0:T(8,128)S(1)} %get-tuple-element.13.delta_ref, ...), custom_call_target="tpu_custom_call" | custom-call | flops 671088640 | bytes 1572864 | tf_op jit(solution)/shard_map/attention_backward/pallas_call | solution.py:212
  30.4 1.9 %collective-permute-start.1 = (bf16[256,512]{1,0:T(8,128)(2,1)S(1)}, bf16[256,512]{1,0:T(8,128)(2,1)S(1)}, u32[]{:S(2)}, u32[]{:S(2)}) collective-permute-start(bf16[256,512]{1,0:T(8,128)(2,1)S(1)} %get-tuple-element.17), channel_id=1, source_target_pairs={{0,1},{1,0},{2,3},{3,2},{4,5},{5,4},{6,7},{7,6},{8,9},{9,8},{10,11... | collective-permute-start | bytes 786440 | tf_op jit(solution)/shard_map/ppermute | solution.py:290
  32.3 0.0 collective-permute-done.kv_ref
  32.3 2.2 %attention_backward.3 = (bf16[128,2048]{1,0:T(8,128)(2,1)S(1)}, f32[256,512]{1,0:T(8,128)S(1)}, bf16[128,4096]{1,0:T(8,128)(2,1)}) custom-call(bf16[128,4096]{1,0:T(8,128)(2,1)S(1)} %bitcast.13, bf16[128,4096]{1,0:T(8,128)(2,1)S(1)} %bitcast.11, f32[32,128]{1,0:T(8,128)S(1)} %bitcast.18, f32[32,128]{1,0:T(8,128)S(1)} %get-tuple-element.13.delta_ref, ...), custom_call_target="tpu_custom_call" | custom-call | flops 671088640 | bytes 1572864 | tf_op jit(solution)/shard_map/attention_backward/pallas_call | solution.py:212
  34.5 0.0 collective-permute-done.1
  34.5 0.1 fusion
  34.6 15.1 %all_to_all.15 = bf16[32,8,512]{2,1,0:T(8,128)(2,1)S(1)} all-to-all(bf16[32,8,512]{2,1,0:T(8,128)(2,1)S(1)} %fusion), channel_id=1, replica_groups=mesh['prompt'=32,'comp'=16] {'prompt'}, dimensions={0} | all-to-all | bytes 524288 | tf_op jit(solution)/shard_map/all_to_all | solution.py:295
  49.7 0.1 reduce_sum.12
  49.7 21.6 %all_to_all.16.parts_ref = bf16[16,8,512]{2,1,0:T(8,128)(2,1)S(1)} all-to-all(bf16[16,8,512]{2,1,0:T(8,128)(2,1)S(1)} %broadcast_in_dim.4), channel_id=1, replica_groups=mesh['prompt'=32,'comp'=16] {'comp'}, dimensions={0} | all-to-all | bytes 262144 | tf_op jit(solution)/shard_map/all_to_all | solution.py:297
  71.3 0.9 %finish.1 = (bf16[8,512]{1,0:T(8,128)(2,1)}, bf16[8,512]{1,0:T(8,128)(2,1)}, bf16[128,4096]{1,0:T(8,128)(2,1)}) custom-call(bf16[16,8,512]{2,1,0:T(8,128)(2,1)S(1)} %all_to_all.16.parts_ref, bf16[128,2048]{1,0:T(8,128)(2,1)S(1)} %get-tuple-element.18.far_ref, bf16[128,4096]{1,0:T(8,128)(2,1)} %get-tuple-element.19.before_hbm), custom_call_target="tpu_custom_call", output_to_operand_aliasing={{2}: (2, {})} | custom-call | tf_op jit(solution)/shard_map/finish/pallas_call | solution.py:249
  (1 shorter events, 0.0 us)
Async XLA Ops:
  2.1 26.1 %copy-start.4 = (f32[1,32,128]{2,1,0:T(8,128)S(1)}, f32[1,32,128]{2,1,0:T(8,128)}, u32[]{:S(2)}) copy-start(f32[1,32,128]{2,1,0:T(8,128)} %param.10) | copy-start | bytes 49156
  2.1 21.7 %all-to-all-start = ((bf16[32,8,512]{2,1,0:T(8,128)(2,1)}), bf16[32,8,512]{2,1,0:T(8,128)(2,1)S(1)}, u32[]{:S(2)}, u32[]{:S(2)}) async-start(bf16[32,8,512]{2,1,0:T(8,128)(2,1)} %spread.1), calls=%async_computation | async-start | bytes 524288 | tf_op jit(solution)/shard_map/all_to_all | solution.py:284
  13.3 1.2 %copy-start = (bf16[1,128,4096]{2,1,0:T(8,128)(2,1)S(1)}, bf16[1,128,4096]{2,1,0:T(8,128)(2,1)}, u32[]{:S(2)}) copy-start(bf16[1,128,4096]{2,1,0:T(8,128)(2,1)} %param.8) | copy-start | bytes 3145732
  14.5 1.2 %copy-start.3 = (bf16[1,128,4096]{2,1,0:T(8,128)(2,1)S(1)}, bf16[1,128,4096]{2,1,0:T(8,128)(2,1)}, u32[]{:S(2)}) copy-start(bf16[1,128,4096]{2,1,0:T(8,128)(2,1)} %param.9) | copy-start | bytes 3145732
  15.7 12.5 %copy-start.1 = (bf16[1,128,4096]{2,1,0:T(8,128)(2,1)S(1)}, bf16[1,128,4096]{2,1,0:T(8,128)(2,1)}, u32[]{:S(2)}) copy-start(bf16[1,128,4096]{2,1,0:T(8,128)(2,1)} %param.8) | copy-start | bytes 3145732
  15.7 12.5 %copy-start.2 = (bf16[1,128,4096]{2,1,0:T(8,128)(2,1)S(1)}, bf16[1,128,4096]{2,1,0:T(8,128)(2,1)}, u32[]{:S(2)}) copy-start(bf16[1,128,4096]{2,1,0:T(8,128)(2,1)} %param.7) | copy-start | bytes 3145732
  23.8 8.5 %collective-permute-start = (bf16[256,512]{1,0:T(8,128)(2,1)S(1)}, bf16[256,512]{1,0:T(8,128)(2,1)S(1)}, u32[]{:S(2)}, u32[]{:S(2)}) collective-permute-start(bf16[256,512]{1,0:T(8,128)(2,1)S(1)} %bitcast.15), channel_id=1, source_target_pairs={{0,1},{1,0},{2,3},{3,2},{4,5},{5,4},{6,7},{7,6},{8,9},{9,8},{10,11... | collective-permute-start | bytes 786440 | tf_op jit(solution)/shard_map/ppermute | solution.py:288
  30.4 4.1 %collective-permute-start.1 = (bf16[256,512]{1,0:T(8,128)(2,1)S(1)}, bf16[256,512]{1,0:T(8,128)(2,1)S(1)}, u32[]{:S(2)}, u32[]{:S(2)}) collective-permute-start(bf16[256,512]{1,0:T(8,128)(2,1)S(1)} %get-tuple-element.17), channel_id=1, source_target_pairs={{0,1},{1,0},{2,3},{3,2},{4,5},{5,4},{6,7},{7,6},{8,9},{9,8},{10,11... | collective-permute-start | bytes 786440 | tf_op jit(solution)/shard_map/ppermute | solution.py:290

commit v4 on v3

--- a/solution.py
+++ b/solution.py
@@ -1,5 +1,3 @@
-import functools
-
 import jax
 import jax.numpy as jnp
 from jax import lax
@@ -8,6 +6,7 @@
 from jax.sharding import PartitionSpec as P
 
 HEAD_SIZE = 128
+SCALE = 1.0 / HEAD_SIZE**0.5
 LOG2_E = 1.4426950408889634
 CORES = 2
 SMALL_VMEM = 8 * 1024 * 1024
@@ -114,7 +113,7 @@
 
 
 def probs_and_dscores(scores, dprobs, rest, delta):
-    scale = LOG2_E / HEAD_SIZE**0.5
+    scale = LOG2_E * SCALE
     rest = rest * LOG2_E
     top = jnp.maximum(jnp.max(scores, axis=0, keepdims=True) * scale, rest)
     weights = jnp.exp2(scores * scale - top)
@@ -144,83 +143,140 @@
     return copies
 
 
-def backward_kernel(turn, q_ref, g_ref, rest_ref, delta_ref, keep_ref, kv_ref, *refs):
-    if turn == 0:
-        dq_ref, dkv_ref = refs
-    else:
-        before_ref, dq_ref, dkv_ref, rows_hbm, sems = refs
-    rows, width = dq_ref.shape
-    half = dkv_ref.shape[1] // 2
-    steps = half // HEAD_SIZE
-    wide = width // steps
+def query_gradients(keys, dscores, rows, dq_ref, at):
+    dq = jnp.dot(keys.T, dscores, preferred_element_type=jnp.float32) * SCALE
+    dq = dq.astype(dq_ref.dtype)
+    for h in range(dq.shape[1] // rows):
+        cut = slice(at + h * HEAD_SIZE, at + (h + 1) * HEAD_SIZE)
+        dq_ref[:, cut] = dq[:, h * rows : (h + 1) * rows].T
+
+
+def key_cuts(width, steps):
+    return [
+        tuple(
+            slice(side * width // 2 + i * HEAD_SIZE, side * width // 2 + (i + 1) * HEAD_SIZE)
+            for side in range(2)
+        )
+        for i in range(steps)
+    ]
+
+
+def softmax_backward(side, steps, kv_ref, q_ref, g_ref, rest_ref, delta_ref, keep_ref):
+    rows = q_ref.shape[0]
+    wide = q_ref.shape[1] // (CORES * steps)
     group = wide // HEAD_SIZE
-    scale = 1.0 / HEAD_SIZE**0.5
-    side = own_core() if turn == 0 else 1 - own_core()
     first = side * steps
-    copies = []
-    if turn == 1:
-        copies = place_half(own_core(), before_ref, rows_hbm, sems)
     keep = keep_ref[...]
-    q, g, p, ds, held = {}, {}, {}, {}, {}
-    for i in range(steps):
+    held = []
+    for i, (key_at, value_at) in enumerate(key_cuts(kv_ref.shape[1], steps)):
         at = pl.multiple_of((first + i) * wide, wide)
         columns = [pl.ds(at + h * HEAD_SIZE, HEAD_SIZE) for h in range(group)]
-        q[i] = jnp.concatenate([q_ref[:, cut] for cut in columns], axis=0)
-        g[i] = jnp.concatenate(
+        q = jnp.concatenate([q_ref[:, cut] for cut in columns], axis=0)
+        g = jnp.concatenate(
             [(g_ref[:, cut].astype(jnp.float32) * keep).astype(jnp.bfloat16) for cut in columns],
             axis=0,
         )
-        key_at = slice(i * HEAD_SIZE, (i + 1) * HEAD_SIZE)
-        value_at = slice(half + i * HEAD_SIZE, half + (i + 1) * HEAD_SIZE)
-        held[i] = scores_and_dprobs(kv_ref[:, key_at], kv_ref[:, value_at], q[i], g[i])
-    for i in range(steps):
+        held.append((q, g, *scores_and_dprobs(kv_ref[:, key_at], kv_ref[:, value_at], q, g)))
+    for i, (q, g, scores, dprobs) in enumerate(held):
         own = pl.ds(pl.multiple_of((first + i) * group, group), group)
-        p[i], ds[i] = probs_and_dscores(
-            *held[i], side_by_side(rest_ref[own, :]), side_by_side(delta_ref[own, :])
-        )
-        keys = kv_ref[:, i * HEAD_SIZE : (i + 1) * HEAD_SIZE]
-        dq = jnp.dot(keys.T, ds[i], preferred_element_type=jnp.float32) * scale
-        dq = dq.astype(jnp.bfloat16)
-        for h in range(group):
-            cut = slice(i * wide + h * HEAD_SIZE, i * wide + (h + 1) * HEAD_SIZE)
-            dq_ref[:, cut] = dq[:, h * rows : (h + 1) * rows].T
-    for i in range(steps):
-        key_terms = jnp.dot(ds[i], q[i], preferred_element_type=jnp.float32) * scale
-        value_terms = jnp.dot(p[i], g[i], preferred_element_type=jnp.float32)
-        dkv_ref[:, i * HEAD_SIZE : (i + 1) * HEAD_SIZE] = key_terms.astype(dkv_ref.dtype)
-        dkv_ref[:, half + i * HEAD_SIZE : half + (i + 1) * HEAD_SIZE] = value_terms.astype(
-            dkv_ref.dtype
-        )
+        yield q, g, *probs_and_dscores(
+            scores, dprobs, side_by_side(rest_ref[own, :]), side_by_side(delta_ref[own, :])
+        )
+
+
+def near_kernel(
+    q_ref, g_ref, rest_ref, delta_ref, keep_ref, kv_ref, packet_ref, dscores_ref
+):
+    prompt, width = kv_ref.shape
+    steps = width // (2 * HEAD_SIZE)
+    wide = dscores_ref.shape[1] // steps
+    packet_ref[:prompt, :] = kv_ref[...]
+    parts = softmax_backward(
+        own_core(), steps, kv_ref, q_ref, g_ref, rest_ref, delta_ref, keep_ref
+    )
+    for i, (q, g, probs, dscores) in enumerate(parts):
+        key_at, value_at = key_cuts(width, steps)[i]
+        dscores_ref[:, i * wide : (i + 1) * wide] = dscores
+        key_terms = jnp.dot(dscores, q, preferred_element_type=jnp.float32) * SCALE
+        value_terms = jnp.dot(probs, g, preferred_element_type=jnp.float32)
+        packet_ref[prompt:, key_at] = key_terms.astype(packet_ref.dtype)
+        packet_ref[prompt:, value_at] = value_terms.astype(packet_ref.dtype)
+
+
+def near_rows_kernel(dscores_ref, kv_ref, dq_ref):
+    rows, width = dq_ref.shape
+    steps = kv_ref.shape[1] // (2 * HEAD_SIZE)
+    wide = width // steps
+    for i, (key_at, _) in enumerate(key_cuts(kv_ref.shape[1], steps)):
+        dscores = dscores_ref[:, i * wide : (i + 1) * wide]
+        query_gradients(kv_ref[:, key_at], dscores, rows, dq_ref, i * wide)
+
+
+def far_kernel(
+    q_ref,
+    g_ref,
+    rest_ref,
+    delta_ref,
+    keep_ref,
+    packet_ref,
+    near_ref,
+    dq_ref,
+    terms_ref,
+    rows_hbm,
+    sems,
+):
+    copies = place_half(own_core(), near_ref, rows_hbm, sems)
+    prompt, width = terms_ref.shape
+    rows = dq_ref.shape[0]
+    steps = width // (2 * HEAD_SIZE)
+    wide = dq_ref.shape[1] // steps
+    kv_ref = packet_ref.at[:prompt, :]
+    parts = softmax_backward(
+        1 - own_core(), steps, kv_ref, q_ref, g_ref, rest_ref, delta_ref, keep_ref
+    )
+    for i, (q, g, probs, dscores) in enumerate(parts):
+        key_at, value_at = key_cuts(width, steps)[i]
+        query_gradients(kv_ref[:, key_at], dscores, rows, dq_ref, i * wide)
+        key_terms = jnp.dot(dscores, q, preferred_element_type=jnp.float32) * SCALE
+        value_terms = jnp.dot(probs, g, preferred_element_type=jnp.float32)
+        terms_ref[:, key_at] = key_terms
+        terms_ref[:, value_at] = value_terms
     for copy in copies:
         copy.wait()
 
 
-def half_gradients(turn, queries, grad_out, rest, delta, keep, kv, *before):
-    rows, width = queries.shape
-    products = rows * (rest.shape[0] // CORES) * kv.shape[0]
+def call(kernel, name, flops, out_shape, *operands, in_float32=(), in_hbm=(), scratch=()):
     vmem = pl.BlockSpec(memory_space=pltpu.VMEM)
-    out_specs = [vmem, vmem]
-    out_shape = [
-        jax.ShapeDtypeStruct((rows, width // CORES), queries.dtype),
-        jax.ShapeDtypeStruct(kv.shape, jnp.float32 if turn else jnp.bfloat16),
-    ]
-    scratch = []
-    if turn == 1:
-        out_specs.append(pl.BlockSpec(memory_space=pltpu.HBM))
-        out_shape.append(jax.ShapeDtypeStruct(queries.shape, queries.dtype))
-        scratch.append(pltpu.SemaphoreType.DMA((PIECES,)))
+    hbm = pl.BlockSpec(memory_space=pltpu.HBM)
     return pl.pallas_call(
-        functools.partial(backward_kernel, turn),
-        in_specs=[vmem] * (6 + len(before)),
-        out_specs=out_specs,
-        out_shape=out_shape,
-        scratch_shapes=scratch,
+        kernel,
+        in_specs=[vmem] * len(operands),
+        out_specs=[hbm if i in in_hbm else vmem for i in range(len(out_shape))],
+        out_shape=[
+            jax.ShapeDtypeStruct(shape, jnp.float32 if i in in_float32 else jnp.bfloat16)
+            for i, shape in enumerate(out_shape)
+        ],
+        scratch_shapes=list(scratch),
         compiler_params=pltpu.CompilerParams(vmem_limit_bytes=LARGE_VMEM),
-        cost_estimate=pl.CostEstimate(
-            flops=10 * products * HEAD_SIZE, bytes_accessed=3 * rows * width, transcendentals=products
-        ),
-        name="attention_backward",
-    )(queries, grad_out, rest, delta, keep, kv, *before)
+        cost_estimate=pl.CostEstimate(flops=flops, bytes_accessed=2**20, transcendentals=0),
+        name=name,
+    )(*operands)
+
+
+def place_half(side, half_ref, rows_hbm, sems):
+    width = half_ref.shape[1]
+    pieces = sems.shape[0]
+    piece = width // pieces
+    copies = []
+    for i in range(pieces):
+        to = pl.ds(pl.multiple_of(side * width + i * piece, piece), piece)
+        copies.append(
+            pltpu.make_async_copy(
+                half_ref.at[:, i * piece : (i + 1) * piece], rows_hbm.at[:, to], sems.at[i]
+            )
+        )
+        copies[-1].start()
+    return copies
 
 
 def finish_kernel(
@@ -285,13 +341,34 @@
         spread(shared_prompt_keys, shared_prompt_values, owners), "prompt", 0, 0
     ).reshape(owners * own, kv_width)
     delta, keep = row_delta(live, grad_out[0], outputs[0], heads, kv_width // HEAD_SIZE)
-    far = lax.ppermute(near, "comp", other_core)
-    grad_near, sent = half_gradients(0, queries[0], grad_out[0], rest, delta, keep, near)
-    received = lax.ppermute(sent, "comp", other_core)
-    grad_far, kept, grad_rows = half_gradients(
-        1, queries[0], grad_out[0], rest, delta, keep, far, grad_near
-    )
-    terms = (kept + received.astype(jnp.float32)).astype(jnp.bfloat16)
+    width = queries.shape[2]
+    half = (rows, width // CORES)
+    prompt = near.shape[0]
+    product = rows * width // CORES * prompt * 2
+    given = (queries[0], grad_out[0], rest, delta, keep)
+    packet, dscores = call(
+        near_kernel,
+        "near",
+        4 * product,
+        [(2 * prompt, kv_width), (prompt, width // CORES)],
+        *given,
+        near,
+    )
+    received = lax.ppermute(packet, "comp", other_core)
+    (grad_near,) = call(near_rows_kernel, "near_rows", product, [half], dscores, near)
+    grad_far, kept, grad_rows = call(
+        far_kernel,
+        "far",
+        5 * product,
+        [half, near.shape, (rows, width)],
+        *given,
+        received,
+        grad_near,
+        in_float32=(1,),
+        in_hbm=(2,),
+        scratch=[pltpu.SemaphoreType.DMA((PIECES,))],
+    )
+    terms = (kept + received[prompt:].astype(jnp.float32)).astype(jnp.bfloat16)
     shares = lax.all_to_all(terms.reshape(owners, own, kv_width), "prompt", 0, 0)
     share = jnp.sum(shares.astype(jnp.float32), axis=0).astype(jnp.bfloat16)
     parts = lax.all_to_all(

time: 72.6 us -> 72 us (level)
  starting transfers between devices: 16.8 us -> 14.9 us
  waiting for transfers between devices: 6.96 us -> 8.05 us
    ppermute x2 -> x1, starting transfers between devices: 6.27 us -> 4.36 us  [shards(): received = lax.ppermute(packet, 'comp', other_core)]
    ppermute x2 -> x1, waiting for transfers between devices: 0.01 us -> 1.1 us  [shards(): received = lax.ppermute(packet, 'comp', other_core)]
    pallas_call x2 -> x3, Pallas kernels: 4.32 us -> 4.47 us  [call(): pl.pallas_call(kernel, in_specs=[vmem] * len(operands), out_specs=[hbm if...]
  transfers between devices with their start and end apart: 3 -> 2, of which waited for: 1 -> 2; matrix products, arithmetic and copies ran while one was open for 0% -> 0% of each run, Pallas kernels for 8% -> 2%
where the time goes in v4:
time: 72 us; the launch traced here: 71.6 us
  blocking collectives  36.8 us (51%)
  starting transfers between devices  14.9 us (21%)
  waiting for transfers between devices  8.05 us (11%)
  Pallas kernels  7.91 us (11%)
  local copies, waits for them, and re-layouts  2.47 us (3%)
  between operations  1.36 us (2%)
    all_to_all x1, blocking collectives, shards(): lax.all_to_all(jnp.broadcast_to(share[None], (members, own, kv_width)), '...  21.6 us
    all_to_all x1, blocking collectives, shards(): lax.all_to_all(terms.reshape(owners, own, kv_width), 'prompt', 0, 0)  15.2 us
    all_to_all x1, starting transfers between devices, shards(): lax.all_to_all(spread(shared_prompt_keys, shared_prompt_values, owners),...  10.5 us
    all_to_all x1, waiting for transfers between devices, shards(): lax.all_to_all(spread(shared_prompt_keys, shared_prompt_values, owners),...  6.95 us
    pallas_call x3, Pallas kernels, call(): pl.pallas_call(kernel, in_specs=[vmem] * len(operands), out_specs=[hbm if...  4.47 us
    ppermute x1, starting transfers between devices, shards(): received = lax.ppermute(packet, 'comp', other_core)  4.36 us
    unnamed x10, local copies, waits for them, and re-layouts  2.46 us
    pallas_call x1, Pallas kernels, spread(): pl.pallas_call(spread_kernel, in_specs=[hbm, hbm], out_specs=hbm, out_sha...  1.46 us
  transfers between devices with their start and end apart: 2, of which 2 were waited for; matrix products, arithmetic and copies ran while one was open for 0% of the time, Pallas kernels for 2%

profile of v4, /device:TPU:1, one launch (start us, length us, event | category | flops | bytes accessed | tf_op | source)
XLA Modules:
  0.0 71.6 jit_solution(18340865477228416815)
XLA Ops:
  0.6 1.5 %spread.1 = bf16[32,8,512]{2,1,0:T(8,128)(2,1)} custom-call(bf16[8,512]{1,0:T(8,128)(2,1)} %k_hbm.1, bf16[8,512]{1,0:T(8,128)(2,1)} %v_hbm.1), custom_call_target="tpu_custom_call" | custom-call | tf_op jit(solution)/shard_map/spread/pallas_call | solution.py:55
  2.1 0.0 copy-start.4
  2.1 10.5 %all-to-all-start = ((bf16[32,8,512]{2,1,0:T(8,128)(2,1)}), bf16[32,8,512]{2,1,0:T(8,128)(2,1)S(1)}, u32[]{:S(2)}, u32[]{:S(2)}) async-start(bf16[32,8,512]{2,1,0:T(8,128)(2,1)} %spread.1), calls=%async_computation | async-start | bytes 524288 | tf_op jit(solution)/shard_map/all_to_all | solution.py:340
  13.3 0.0 copy-start
  13.3 1.2 %copy-done = bf16[1,128,4096]{2,1,0:T(8,128)(2,1)S(1)} copy-done((bf16[1,128,4096]{2,1,0:T(8,128)(2,1)S(1)}, bf16[1,128,4096]{2,1,0:T(8,128)(2,1)}, u32[]{:S(2)}) %copy-start) | copy-done | bytes 1048600
  14.5 0.0 copy-start.3
  14.5 1.2 %copy-done.3 = bf16[1,128,4096]{2,1,0:T(8,128)(2,1)S(1)} copy-done((bf16[1,128,4096]{2,1,0:T(8,128)(2,1)S(1)}, bf16[1,128,4096]{2,1,0:T(8,128)(2,1)}, u32[]{:S(2)}) %copy-start.3) | copy-done | bytes 1048600
  15.7 0.0 copy-start.1
  15.7 0.0 copy-start.2
  15.7 1.1 %delta.1 = (f32[32,128]{1,0:T(8,128)S(1)}, f32[128,128]{1,0:T(8,128)S(1)}) custom-call(s32[1]{0:T(128)S(6)} %sub.7.live_ref, bf16[128,4096]{1,0:T(8,128)(2,1)S(1)} %bitcast.9, bf16[128,4096]{1,0:T(8,128)(2,1)S(1)} %bitcast.16), custom_call_target="tpu_custom_call" | custom-call | flops 1572864 | bytes 2097152 | tf_op jit(solution)/shard_map/delta/pallas_call | solution.py:90
  16.9 7.0 %all-to-all-done = bf16[32,8,512]{2,1,0:T(8,128)(2,1)S(1)} async-done(((bf16[32,8,512]{2,1,0:T(8,128)(2,1)}), bf16[32,8,512]{2,1,0:T(8,128)(2,1)S(1)}, u32[]{:S(2)}, u32[]{:S(2)}) %all-to-all-start) | async-done | bytes 262176 | tf_op jit(solution)/shard_map/all_to_all | solution.py:340
  23.8 0.0 copy-done.4
  23.8 0.0 copy-done.1
  23.8 0.0 copy-done.2
  23.8 2.0 %near.1 = (bf16[512,512]{1,0:T(8,128)(2,1)S(1)}, bf16[256,2048]{1,0:T(8,128)(2,1)S(1)}) custom-call(bf16[128,4096]{1,0:T(8,128)(2,1)S(1)} %bitcast.12, bf16[128,4096]{1,0:T(8,128)(2,1)S(1)} %bitcast.10, f32[32,128]{1,0:T(8,128)S(1)} %bitcast.17, f32[32,128]{1,0:T(8,128)S(1)} %get-tuple-element.13.delta_ref, f32[128,128]{1,0:T(8,128)S(1)} %get-tuple-element.14.keep_ref, ...), custom_call_target="tpu_custom_call" | custom-call | flops 536870912 | bytes 1048576 | tf_op jit(solution)/shard_map/near/pallas_call | solution.py:251
  25.8 4.4 %collective-permute-start = (bf16[512,512]{1,0:T(8,128)(2,1)S(1)}, bf16[512,512]{1,0:T(8,128)(2,1)S(1)}, u32[]{:S(2)}, u32[]{:S(2)}) collective-permute-start(bf16[512,512]{1,0:T(8,128)(2,1)S(1)} %get-tuple-element.15), channel_id=1, source_target_pairs={{0,1},{1,0},{2,3},{3,2},{4,5},{5,4},{6,7},{7,6},{8,9},{9,8},{10,11... | collective-permute-start | bytes 1572872 | tf_op jit(solution)/shard_map/ppermute | solution.py:357
  30.2 0.4 near_rows.1.near_ref
  30.6 1.1 %collective-permute-done.packet_ref = bf16[512,512]{1,0:T(8,128)(2,1)S(1)} collective-permute-done((bf16[512,512]{1,0:T(8,128)(2,1)S(1)}, bf16[512,512]{1,0:T(8,128)(2,1)S(1)}, u32[]{:S(2)}, u32[]{:S(2)}) %collective-permute-start) | collective-permute-done | bytes 524320 | tf_op jit(solution)/shard_map/ppermute | solution.py:357
  31.7 2.1 %far.1 = (bf16[128,2048]{1,0:T(8,128)(2,1)S(1)}, f32[256,512]{1,0:T(8,128)S(1)}, bf16[128,4096]{1,0:T(8,128)(2,1)}) custom-call(bf16[128,4096]{1,0:T(8,128)(2,1)S(1)} %bitcast.13, bf16[128,4096]{1,0:T(8,128)(2,1)S(1)} %bitcast.11, f32[32,128]{1,0:T(8,128)S(1)} %bitcast.18, f32[32,128]{1,0:T(8,128)S(1)} %get-tuple-element.13.delta_ref, ...), custom_call_target="tpu_custom_call" | custom-call | flops 671088640 | bytes 1048576 | tf_op jit(solution)/shard_map/far/pallas_call | solution.py:251
  33.8 0.1 fusion
  33.9 15.2 %all_to_all.15 = bf16[32,8,512]{2,1,0:T(8,128)(2,1)S(1)} all-to-all(bf16[32,8,512]{2,1,0:T(8,128)(2,1)S(1)} %fusion), channel_id=1, replica_groups=mesh['prompt'=32,'comp'=16] {'prompt'}, dimensions={0} | all-to-all | bytes 524288 | tf_op jit(solution)/shard_map/all_to_all | solution.py:372
  49.0 0.1 reduce_sum.12
  49.1 21.6 %all_to_all.16.parts_ref = bf16[16,8,512]{2,1,0:T(8,128)(2,1)S(1)} all-to-all(bf16[16,8,512]{2,1,0:T(8,128)(2,1)S(1)} %broadcast_in_dim.4), channel_id=1, replica_groups=mesh['prompt'=32,'comp'=16] {'comp'}, dimensions={0} | all-to-all | bytes 262144 | tf_op jit(solution)/shard_map/all_to_all | solution.py:374
  70.7 0.9 %finish.1 = (bf16[8,512]{1,0:T(8,128)(2,1)}, bf16[8,512]{1,0:T(8,128)(2,1)}, bf16[128,4096]{1,0:T(8,128)(2,1)}) custom-call(bf16[16,8,512]{2,1,0:T(8,128)(2,1)S(1)} %all_to_all.16.parts_ref, bf16[128,2048]{1,0:T(8,128)(2,1)S(1)} %get-tuple-element.18.far_ref, bf16[128,4096]{1,0:T(8,128)(2,1)} %get-tuple-element.19.before_hbm), custom_call_target="tpu_custom_call", output_to_operand_aliasing={{2}: (2, {})} | custom-call | tf_op jit(solution)/shard_map/finish/pallas_call | solution.py:305
  (1 shorter events, 0.0 us)
Async XLA Ops:
  2.1 21.7 %copy-start.4 = (f32[1,32,128]{2,1,0:T(8,128)S(1)}, f32[1,32,128]{2,1,0:T(8,128)}, u32[]{:S(2)}) copy-start(f32[1,32,128]{2,1,0:T(8,128)} %param.10) | copy-start | bytes 49156
  2.1 21.7 %all-to-all-start = ((bf16[32,8,512]{2,1,0:T(8,128)(2,1)}), bf16[32,8,512]{2,1,0:T(8,128)(2,1)S(1)}, u32[]{:S(2)}, u32[]{:S(2)}) async-start(bf16[32,8,512]{2,1,0:T(8,128)(2,1)} %spread.1), calls=%async_computation | async-start | bytes 524288 | tf_op jit(solution)/shard_map/all_to_all | solution.py:340
  13.3 1.2 %copy-start = (bf16[1,128,4096]{2,1,0:T(8,128)(2,1)S(1)}, bf16[1,128,4096]{2,1,0:T(8,128)(2,1)}, u32[]{:S(2)}) copy-start(bf16[1,128,4096]{2,1,0:T(8,128)(2,1)} %param.8) | copy-start | bytes 3145732
  14.5 1.2 %copy-start.3 = (bf16[1,128,4096]{2,1,0:T(8,128)(2,1)S(1)}, bf16[1,128,4096]{2,1,0:T(8,128)(2,1)}, u32[]{:S(2)}) copy-start(bf16[1,128,4096]{2,1,0:T(8,128)(2,1)} %param.9) | copy-start | bytes 3145732
  15.7 8.1 %copy-start.1 = (bf16[1,128,4096]{2,1,0:T(8,128)(2,1)S(1)}, bf16[1,128,4096]{2,1,0:T(8,128)(2,1)}, u32[]{:S(2)}) copy-start(bf16[1,128,4096]{2,1,0:T(8,128)(2,1)} %param.8) | copy-start | bytes 3145732
  15.7 8.1 %copy-start.2 = (bf16[1,128,4096]{2,1,0:T(8,128)(2,1)S(1)}, bf16[1,128,4096]{2,1,0:T(8,128)(2,1)}, u32[]{:S(2)}) copy-start(bf16[1,128,4096]{2,1,0:T(8,128)(2,1)} %param.7) | copy-start | bytes 3145732
  25.8 5.9 %collective-permute-start = (bf16[512,512]{1,0:T(8,128)(2,1)S(1)}, bf16[512,512]{1,0:T(8,128)(2,1)S(1)}, u32[]{:S(2)}, u32[]{:S(2)}) collective-permute-start(bf16[512,512]{1,0:T(8,128)(2,1)S(1)} %get-tuple-element.15), channel_id=1, source_target_pairs={{0,1},{1,0},{2,3},{3,2},{4,5},{5,4},{6,7},{7,6},{8,9},{9,8},{10,11... | collective-permute-start | bytes 1572872 | tf_op jit(solution)/shard_map/ppermute | solution.py:357

commit v5 on v4

--- a/solution.py
+++ b/solution.py
@@ -23,46 +23,19 @@
     return lax.rem(lax.axis_index("comp"), CORES)
 
 
-def spread_kernel(k_hbm, v_hbm, out_hbm, half_buf, out_buf, in_sems, out_sems):
-    half = half_buf.shape[2]
+def spread_kernel(k_ref, v_ref, out_ref):
+    half = k_ref.shape[1] // CORES
     at = pl.ds(pl.multiple_of(own_core() * half, half), half)
-    loads = [
-        pltpu.make_async_copy(ref.at[:, at], half_buf.at[i], in_sems.at[i])
-        for i, ref in enumerate((k_hbm, v_hbm))
-    ]
-    for copy in loads:
-        copy.start()
-    for copy in loads:
-        copy.wait()
-    both = jnp.concatenate([half_buf[0], half_buf[1]], axis=1)
-    pieces = out_sems.shape[0]
-    piece = out_buf.shape[0] // pieces
-    stores = []
-    for i in range(pieces):
-        for j in range(piece):
-            out_buf[i * piece + j] = both
-        own = pl.ds(i * piece, piece)
-        stores.append(pltpu.make_async_copy(out_buf.at[own], out_hbm.at[own], out_sems.at[i]))
-        stores[-1].start()
-    for copy in stores:
-        copy.wait()
+    both = jnp.concatenate([k_ref[:, at], v_ref[:, at]], axis=1)
+    for i in range(out_ref.shape[0]):
+        out_ref[i] = both
 
 
 def spread(keys, values, owners):
     own, width = keys.shape
-    hbm = pl.BlockSpec(memory_space=pltpu.HBM)
-    shape = (owners, own, 2 * width // CORES)
     return pl.pallas_call(
         spread_kernel,
-        in_specs=[hbm, hbm],
-        out_specs=hbm,
-        out_shape=jax.ShapeDtypeStruct(shape, keys.dtype),
-        scratch_shapes=[
-            pltpu.VMEM((2, own, width // CORES), keys.dtype),
-            pltpu.VMEM(shape, keys.dtype),
-            pltpu.SemaphoreType.DMA((2,)),
-            pltpu.SemaphoreType.DMA((4,)),
-        ],
+        out_shape=jax.ShapeDtypeStruct((owners, own, 2 * width // CORES), keys.dtype),
         compiler_params=pltpu.CompilerParams(vmem_limit_bytes=FULL_VMEM),
         name="spread",
     )(keys, values)
@@ -279,40 +252,35 @@
     return copies
 
 
-def finish_kernel(
-    parts_ref, far_ref, before_hbm, key_hbm, value_hbm, rows_hbm, key_buf, value_buf, sems, out_sems
-):
-    copies = place_half(1 - own_core(), far_ref, rows_hbm, sems)
-    half = parts_ref.shape[2] // 2
-    for core in range(CORES):
-        total = parts_ref[core].astype(jnp.float32)
-        for i in range(core + CORES, parts_ref.shape[0], CORES):
-            total += parts_ref[i].astype(jnp.float32)
-        at = slice((CORES - 1 - core) * half, (CORES - core) * half)
-        key_buf[:, at] = total[:, :half].astype(key_buf.dtype)
-        value_buf[:, at] = total[:, half:].astype(value_buf.dtype)
-    for i, (buf, hbm) in enumerate(((key_buf, key_hbm), (value_buf, value_hbm))):
-        copies.append(pltpu.make_async_copy(buf, hbm, out_sems.at[i]))
-        copies[-1].start()
-    for copy in copies:
-        copy.wait()
+def finish_kernel(parts_ref, far_ref, before_hbm, key_ref, value_ref, rows_ref):
+    turn = pl.program_id(0)
+    first = CORES - 1 - turn
+    total = parts_ref[first].astype(jnp.float32)
+    for i in range(CORES, parts_ref.shape[0], CORES):
+        total += parts_ref[first + i].astype(jnp.float32)
+    half = total.shape[1] // 2
+    key_ref[...] = total[:, :half].astype(key_ref.dtype)
+    value_ref[...] = total[:, half:].astype(value_ref.dtype)
+    width = rows_ref.shape[1]
+    rows_ref[...] = far_ref[:, pl.ds(pl.multiple_of(turn * width, width), width)]
 
 
 def finish(parts, far, grad_rows, like):
     vmem = pl.BlockSpec(memory_space=pltpu.VMEM)
     hbm = pl.BlockSpec(memory_space=pltpu.HBM)
     one = jax.ShapeDtypeStruct(like.shape, like.dtype)
+    own, width = like.shape
+    piece = (far.shape[0], far.shape[1] // CORES)
     return pl.pallas_call(
         finish_kernel,
+        grid=(CORES,),
         in_specs=[vmem, vmem, hbm],
-        out_specs=[hbm, hbm, hbm],
+        out_specs=[
+            pl.BlockSpec((own, width // CORES), lambda i: (0, i)),
+            pl.BlockSpec((own, width // CORES), lambda i: (0, i)),
+            pl.BlockSpec(piece, lambda i: (0, (1 - own_core()) * CORES + i)),
+        ],
         out_shape=[one, one, jax.ShapeDtypeStruct(grad_rows.shape, grad_rows.dtype)],
-        scratch_shapes=[
-            pltpu.VMEM(like.shape, like.dtype),
-            pltpu.VMEM(like.shape, like.dtype),
-            pltpu.SemaphoreType.DMA((PIECES,)),
-            pltpu.SemaphoreType.DMA((2,)),
-        ],
         input_output_aliases={2: 2},
         compiler_params=pltpu.CompilerParams(vmem_limit_bytes=SMALL_VMEM),
         name="finish",

time: 72 us -> 72.1 us (level)
  no operation moved by 1% of the time
where the time goes in v5:
time: 72.1 us; the launch traced here: 71.6 us
  blocking collectives  36.8 us (51%)
  starting transfers between devices  15 us (21%)
  waiting for transfers between devices  8.05 us (11%)
  Pallas kernels  7.84 us (11%)
  local copies, waits for them, and re-layouts  2.47 us (3%)
  between operations  1.35 us (2%)
    all_to_all x1, blocking collectives, shards(): lax.all_to_all(jnp.broadcast_to(share[None], (members, own, kv_width)), '...  21.6 us
    all_to_all x1, blocking collectives, shards(): lax.all_to_all(terms.reshape(owners, own, kv_width), 'prompt', 0, 0)  15.2 us
    all_to_all x1, starting transfers between devices, shards(): lax.all_to_all(spread(shared_prompt_keys, shared_prompt_values, owners),...  10.6 us
    all_to_all x1, waiting for transfers between devices, shards(): lax.all_to_all(spread(shared_prompt_keys, shared_prompt_values, owners),...  6.95 us
    pallas_call x3, Pallas kernels, call(): pl.pallas_call(kernel, in_specs=[vmem] * len(operands), out_specs=[hbm if...  4.45 us
    ppermute x1, starting transfers between devices, shards(): received = lax.ppermute(packet, 'comp', other_core)  4.38 us
    unnamed x10, local copies, waits for them, and re-layouts  2.46 us
  transfers between devices with their start and end apart: 2, of which 2 were waited for; matrix products, arithmetic and copies ran while one was open for 0% of the time, Pallas kernels for 2%

profile of v5, /device:TPU:1, one launch (start us, length us, event | category | flops | bytes accessed | tf_op | source)
XLA Modules:
  0.0 71.6 jit_solution(9441707127947767205)
XLA Ops:
  0.6 1.4 %spread.1 = bf16[32,8,512]{2,1,0:T(8,128)(2,1)} custom-call(bf16[8,512]{1,0:T(8,128)(2,1)} %k_ref.1, bf16[8,512]{1,0:T(8,128)(2,1)} %v_ref.1), custom_call_target="tpu_custom_call" | custom-call | tf_op jit(solution)/shard_map/spread/pallas_call | solution.py:36
  2.1 0.0 copy-start.4
  2.1 10.6 %all-to-all-start = ((bf16[32,8,512]{2,1,0:T(8,128)(2,1)}), bf16[32,8,512]{2,1,0:T(8,128)(2,1)S(1)}, u32[]{:S(2)}, u32[]{:S(2)}) async-start(bf16[32,8,512]{2,1,0:T(8,128)(2,1)} %spread.1), calls=%async_computation | async-start | bytes 524288 | tf_op jit(solution)/shard_map/all_to_all | solution.py:308
  13.4 0.0 copy-start
  13.4 1.2 %copy-done = bf16[1,128,4096]{2,1,0:T(8,128)(2,1)S(1)} copy-done((bf16[1,128,4096]{2,1,0:T(8,128)(2,1)S(1)}, bf16[1,128,4096]{2,1,0:T(8,128)(2,1)}, u32[]{:S(2)}) %copy-start) | copy-done | bytes 1048600
  14.6 0.0 copy-start.3
  14.6 1.2 %copy-done.3 = bf16[1,128,4096]{2,1,0:T(8,128)(2,1)S(1)} copy-done((bf16[1,128,4096]{2,1,0:T(8,128)(2,1)S(1)}, bf16[1,128,4096]{2,1,0:T(8,128)(2,1)}, u32[]{:S(2)}) %copy-start.3) | copy-done | bytes 1048600
  15.8 0.0 copy-start.1
  15.8 0.0 copy-start.2
  15.8 1.1 %delta.1 = (f32[32,128]{1,0:T(8,128)S(1)}, f32[128,128]{1,0:T(8,128)S(1)}) custom-call(s32[1]{0:T(128)S(6)} %sub.7.live_ref, bf16[128,4096]{1,0:T(8,128)(2,1)S(1)} %bitcast.9, bf16[128,4096]{1,0:T(8,128)(2,1)S(1)} %bitcast.16), custom_call_target="tpu_custom_call" | custom-call | flops 1572864 | bytes 2097152 | tf_op jit(solution)/shard_map/delta/pallas_call | solution.py:63
  16.9 7.0 %all-to-all-done = bf16[32,8,512]{2,1,0:T(8,128)(2,1)S(1)} async-done(((bf16[32,8,512]{2,1,0:T(8,128)(2,1)}), bf16[32,8,512]{2,1,0:T(8,128)(2,1)S(1)}, u32[]{:S(2)}, u32[]{:S(2)}) %all-to-all-start) | async-done | bytes 262176 | tf_op jit(solution)/shard_map/all_to_all | solution.py:308
  23.9 0.0 copy-done.4
  23.9 0.0 copy-done.1
  23.9 0.0 copy-done.2
  23.9 2.0 %near.1 = (bf16[512,512]{1,0:T(8,128)(2,1)S(1)}, bf16[256,2048]{1,0:T(8,128)(2,1)S(1)}) custom-call(bf16[128,4096]{1,0:T(8,128)(2,1)S(1)} %bitcast.12, bf16[128,4096]{1,0:T(8,128)(2,1)S(1)} %bitcast.10, f32[32,128]{1,0:T(8,128)S(1)} %bitcast.17, f32[32,128]{1,0:T(8,128)S(1)} %get-tuple-element.13.delta_ref, f32[128,128]{1,0:T(8,128)S(1)} %get-tuple-element.14.keep_ref, ...), custom_call_target="tpu_custom_call" | custom-call | flops 536870912 | bytes 1048576 | tf_op jit(solution)/shard_map/near/pallas_call | solution.py:224
  25.9 4.4 %collective-permute-start = (bf16[512,512]{1,0:T(8,128)(2,1)S(1)}, bf16[512,512]{1,0:T(8,128)(2,1)S(1)}, u32[]{:S(2)}, u32[]{:S(2)}) collective-permute-start(bf16[512,512]{1,0:T(8,128)(2,1)S(1)} %get-tuple-element.15), channel_id=1, source_target_pairs={{0,1},{1,0},{2,3},{3,2},{4,5},{5,4},{6,7},{7,6},{8,9},{9,8},{10,11... | collective-permute-start | bytes 1572872 | tf_op jit(solution)/shard_map/ppermute | solution.py:325
  30.3 0.4 near_rows.1.near_ref
  30.7 1.1 %collective-permute-done.packet_ref = bf16[512,512]{1,0:T(8,128)(2,1)S(1)} collective-permute-done((bf16[512,512]{1,0:T(8,128)(2,1)S(1)}, bf16[512,512]{1,0:T(8,128)(2,1)S(1)}, u32[]{:S(2)}, u32[]{:S(2)}) %collective-permute-start) | collective-permute-done | bytes 524320 | tf_op jit(solution)/shard_map/ppermute | solution.py:325
  31.8 2.1 %far.1 = (bf16[128,2048]{1,0:T(8,128)(2,1)S(1)}, f32[256,512]{1,0:T(8,128)S(1)}, bf16[128,4096]{1,0:T(8,128)(2,1)}) custom-call(bf16[128,4096]{1,0:T(8,128)(2,1)S(1)} %bitcast.13, bf16[128,4096]{1,0:T(8,128)(2,1)S(1)} %bitcast.11, f32[32,128]{1,0:T(8,128)S(1)} %bitcast.18, f32[32,128]{1,0:T(8,128)S(1)} %get-tuple-element.13.delta_ref, ...), custom_call_target="tpu_custom_call" | custom-call | flops 671088640 | bytes 1048576 | tf_op jit(solution)/shard_map/far/pallas_call | solution.py:224
  33.9 0.1 fusion
  33.9 15.2 %all_to_all.15 = bf16[32,8,512]{2,1,0:T(8,128)(2,1)S(1)} all-to-all(bf16[32,8,512]{2,1,0:T(8,128)(2,1)S(1)} %fusion), channel_id=1, replica_groups=mesh['prompt'=32,'comp'=16] {'prompt'}, dimensions={0} | all-to-all | bytes 524288 | tf_op jit(solution)/shard_map/all_to_all | solution.py:340
  49.1 0.1 reduce_sum.12
  49.2 21.6 %all_to_all.16.parts_ref = bf16[16,8,512]{2,1,0:T(8,128)(2,1)S(1)} all-to-all(bf16[16,8,512]{2,1,0:T(8,128)(2,1)S(1)} %broadcast_in_dim.4), channel_id=1, replica_groups=mesh['prompt'=32,'comp'=16] {'comp'}, dimensions={0} | all-to-all | bytes 262144 | tf_op jit(solution)/shard_map/all_to_all | solution.py:342
  70.8 0.8 %finish.1 = (bf16[8,512]{1,0:T(8,128)(2,1)}, bf16[8,512]{1,0:T(8,128)(2,1)}, bf16[128,4096]{1,0:T(8,128)(2,1)}) custom-call(bf16[16,8,512]{2,1,0:T(8,128)(2,1)S(1)} %all_to_all.16.parts_ref, bf16[128,2048]{1,0:T(8,128)(2,1)S(1)} %get-tuple-element.18.far_ref, bf16[128,4096]{1,0:T(8,128)(2,1)} %get-tuple-element.19.before_hbm), custom_call_target="tpu_custom_call", output_to_operand_aliasing={{2}: (2, {})} | custom-call | tf_op jit(solution)/shard_map/finish/pallas_call | solution.py:274
  (1 shorter events, 0.0 us)
Async XLA Ops:
  2.1 21.8 %copy-start.4 = (f32[1,32,128]{2,1,0:T(8,128)S(1)}, f32[1,32,128]{2,1,0:T(8,128)}, u32[]{:S(2)}) copy-start(f32[1,32,128]{2,1,0:T(8,128)} %param.10) | copy-start | bytes 49156
  2.1 21.8 %all-to-all-start = ((bf16[32,8,512]{2,1,0:T(8,128)(2,1)}), bf16[32,8,512]{2,1,0:T(8,128)(2,1)S(1)}, u32[]{:S(2)}, u32[]{:S(2)}) async-start(bf16[32,8,512]{2,1,0:T(8,128)(2,1)} %spread.1), calls=%async_computation | async-start | bytes 524288 | tf_op jit(solution)/shard_map/all_to_all | solution.py:308
  13.4 1.2 %copy-start = (bf16[1,128,4096]{2,1,0:T(8,128)(2,1)S(1)}, bf16[1,128,4096]{2,1,0:T(8,128)(2,1)}, u32[]{:S(2)}) copy-start(bf16[1,128,4096]{2,1,0:T(8,128)(2,1)} %param.8) | copy-start | bytes 3145732
  14.6 1.2 %copy-start.3 = (bf16[1,128,4096]{2,1,0:T(8,128)(2,1)S(1)}, bf16[1,128,4096]{2,1,0:T(8,128)(2,1)}, u32[]{:S(2)}) copy-start(bf16[1,128,4096]{2,1,0:T(8,128)(2,1)} %param.9) | copy-start | bytes 3145732
  15.8 8.1 %copy-start.1 = (bf16[1,128,4096]{2,1,0:T(8,128)(2,1)S(1)}, bf16[1,128,4096]{2,1,0:T(8,128)(2,1)}, u32[]{:S(2)}) copy-start(bf16[1,128,4096]{2,1,0:T(8,128)(2,1)} %param.8) | copy-start | bytes 3145732
  15.8 8.1 %copy-start.2 = (bf16[1,128,4096]{2,1,0:T(8,128)(2,1)S(1)}, bf16[1,128,4096]{2,1,0:T(8,128)(2,1)}, u32[]{:S(2)}) copy-start(bf16[1,128,4096]{2,1,0:T(8,128)(2,1)} %param.7) | copy-start | bytes 3145732
  25.9 5.9 %collective-permute-start = (bf16[512,512]{1,0:T(8,128)(2,1)S(1)}, bf16[512,512]{1,0:T(8,128)(2,1)S(1)}, u32[]{:S(2)}, u32[]{:S(2)}) collective-permute-start(bf16[512,512]{1,0:T(8,128)(2,1)S(1)} %get-tuple-element.15), channel_id=1, source_target_pairs={{0,1},{1,0},{2,3},{3,2},{4,5},{5,4},{6,7},{7,6},{8,9},{9,8},{10,11... | collective-permute-start | bytes 1572872 | tf_op jit(solution)/shard_map/ppermute | solution.py:325

commit v6 on v5

--- a/solution.py
+++ b/solution.py
@@ -41,18 +41,20 @@
     )(keys, values)
 
 
-def delta_kernel(live_ref, g_ref, o_ref, delta_ref, keep_ref):
+def delta_kernel(live_ref, g_ref, o_ref, delta_ref, masked_ref):
     rows, wide = o_ref.shape
     heads = wide // HEAD_SIZE
     step = pl.program_id(0)
-    live = lax.broadcasted_iota(jnp.int32, (rows, HEAD_SIZE), 0) < live_ref[0]
-    keep_ref[...] = live.astype(jnp.float32)
+    keep = lax.broadcasted_iota(jnp.int32, (rows, HEAD_SIZE), 0) < live_ref[0]
+    keep = keep.astype(jnp.float32)
     columns = []
     for h in range(heads):
         cut = slice(h * HEAD_SIZE, (h + 1) * HEAD_SIZE)
         at = pl.ds(pl.multiple_of(step * wide + h * HEAD_SIZE, HEAD_SIZE), HEAD_SIZE)
-        product = g_ref[:, at].astype(jnp.float32) * o_ref[:, cut].astype(jnp.float32)
-        columns.append(jnp.sum(jnp.where(live, product, 0.0), axis=1, keepdims=True))
+        masked = g_ref[:, cut].astype(jnp.float32) * keep
+        masked_ref[:, at] = masked.astype(masked_ref.dtype)
+        product = masked * o_ref[:, cut].astype(jnp.float32)
+        columns.append(jnp.sum(product, axis=1, keepdims=True))
     own = pl.ds(pl.multiple_of(step * heads, heads), heads)
     delta_ref[own, :] = jnp.concatenate(columns, axis=1).T
 
@@ -65,13 +67,13 @@
         grid=(steps,),
         in_specs=[
             pl.BlockSpec(memory_space=pltpu.SMEM),
-            vmem,
+            pl.BlockSpec((rows, width // steps), lambda h: (0, h)),
             pl.BlockSpec((rows, width // steps), lambda h: (0, h)),
         ],
         out_specs=[vmem, vmem],
         out_shape=[
             jax.ShapeDtypeStruct((heads, rows), jnp.float32),
-            jax.ShapeDtypeStruct((rows, HEAD_SIZE), jnp.float32),
+            jax.ShapeDtypeStruct((rows, width), grad_out.dtype),
         ],
         compiler_params=pltpu.CompilerParams(vmem_limit_bytes=SMALL_VMEM),
         cost_estimate=pl.CostEstimate(
@@ -134,21 +136,17 @@
     ]
 
 
-def softmax_backward(side, steps, kv_ref, q_ref, g_ref, rest_ref, delta_ref, keep_ref):
+def softmax_backward(side, steps, kv_ref, q_ref, g_ref, rest_ref, delta_ref):
     rows = q_ref.shape[0]
     wide = q_ref.shape[1] // (CORES * steps)
     group = wide // HEAD_SIZE
     first = side * steps
-    keep = keep_ref[...]
     held = []
     for i, (key_at, value_at) in enumerate(key_cuts(kv_ref.shape[1], steps)):
         at = pl.multiple_of((first + i) * wide, wide)
         columns = [pl.ds(at + h * HEAD_SIZE, HEAD_SIZE) for h in range(group)]
         q = jnp.concatenate([q_ref[:, cut] for cut in columns], axis=0)
-        g = jnp.concatenate(
-            [(g_ref[:, cut].astype(jnp.float32) * keep).astype(jnp.bfloat16) for cut in columns],
-            axis=0,
-        )
+        g = jnp.concatenate([g_ref[:, cut] for cut in columns], axis=0)
         held.append((q, g, *scores_and_dprobs(kv_ref[:, key_at], kv_ref[:, value_at], q, g)))
     for i, (q, g, scores, dprobs) in enumerate(held):
         own = pl.ds(pl.multiple_of((first + i) * group, group), group)
@@ -158,14 +156,14 @@
 
 
 def near_kernel(
-    q_ref, g_ref, rest_ref, delta_ref, keep_ref, kv_ref, packet_ref, dscores_ref
+    q_ref, g_ref, rest_ref, delta_ref, kv_ref, packet_ref, dscores_ref
 ):
     prompt, width = kv_ref.shape
     steps = width // (2 * HEAD_SIZE)
     wide = dscores_ref.shape[1] // steps
     packet_ref[:prompt, :] = kv_ref[...]
     parts = softmax_backward(
-        own_core(), steps, kv_ref, q_ref, g_ref, rest_ref, delta_ref, keep_ref
+        own_core(), steps, kv_ref, q_ref, g_ref, rest_ref, delta_ref
     )
     for i, (q, g, probs, dscores) in enumerate(parts):
         key_at, value_at = key_cuts(width, steps)[i]
@@ -190,7 +188,6 @@
     g_ref,
     rest_ref,
     delta_ref,
-    keep_ref,
     packet_ref,
     near_ref,
     dq_ref,
@@ -205,7 +202,7 @@
     wide = dq_ref.shape[1] // steps
     kv_ref = packet_ref.at[:prompt, :]
     parts = softmax_backward(
-        1 - own_core(), steps, kv_ref, q_ref, g_ref, rest_ref, delta_ref, keep_ref
+        1 - own_core(), steps, kv_ref, q_ref, g_ref, rest_ref, delta_ref
     )
     for i, (q, g, probs, dscores) in enumerate(parts):
         key_at, value_at = key_cuts(width, steps)[i]
@@ -308,12 +305,12 @@
     near = lax.all_to_all(
         spread(shared_prompt_keys, shared_prompt_values, owners), "prompt", 0, 0
     ).reshape(owners * own, kv_width)
-    delta, keep = row_delta(live, grad_out[0], outputs[0], heads, kv_width // HEAD_SIZE)
+    delta, masked = row_delta(live, grad_out[0], outputs[0], heads, kv_width // HEAD_SIZE)
     width = queries.shape[2]
     half = (rows, width // CORES)
     prompt = near.shape[0]
     product = rows * width // CORES * prompt * 2
-    given = (queries[0], grad_out[0], rest, delta, keep)
+    given = (queries[0], masked, rest, delta)
     packet, dscores = call(
         near_kernel,
         "near",

time: 72.1 us -> 71.8 us (level)
    unnamed x10 -> x8, local copies, waits for them, and re-layouts: 2.46 us -> 2.45 us
where the time goes in v6:
time: 71.8 us; the launch traced here: 71.4 us
  blocking collectives  36.8 us (51%)
  starting transfers between devices  14.8 us (21%)
  waiting for transfers between devices  7.98 us (11%)
  Pallas kernels  7.89 us (11%)
  local copies, waits for them, and re-layouts  2.46 us (3%)
  between operations  1.34 us (2%)
    all_to_all x1, blocking collectives, shards(): lax.all_to_all(jnp.broadcast_to(share[None], (members, own, kv_width)), '...  21.6 us
    all_to_all x1, blocking collectives, shards(): lax.all_to_all(terms.reshape(owners, own, kv_width), 'prompt', 0, 0)  15.2 us
    all_to_all x1, starting transfers between devices, shards(): lax.all_to_all(spread(shared_prompt_keys, shared_prompt_values, owners),...  10.5 us
    all_to_all x1, waiting for transfers between devices, shards(): lax.all_to_all(spread(shared_prompt_keys, shared_prompt_values, owners),...  6.88 us
    pallas_call x3, Pallas kernels, call(): pl.pallas_call(kernel, in_specs=[vmem] * len(operands), out_specs=[hbm if...  4.44 us
    ppermute x1, starting transfers between devices, shards(): received = lax.ppermute(packet, 'comp', other_core)  4.34 us
    unnamed x8, local copies, waits for them, and re-layouts  2.45 us
  transfers between devices with their start and end apart: 2, of which 2 were waited for; matrix products, arithmetic and copies ran while one was open for 0% of the time, Pallas kernels for 2%

profile of v6, /device:TPU:1, one launch (start us, length us, event | category | flops | bytes accessed | tf_op | source)
XLA Modules:
  0.0 71.4 jit_solution(16020331253593604835)
XLA Ops:
  0.6 1.4 %spread.1 = bf16[32,8,512]{2,1,0:T(8,128)(2,1)} custom-call(bf16[8,512]{1,0:T(8,128)(2,1)} %k_ref.1, bf16[8,512]{1,0:T(8,128)(2,1)} %v_ref.1), custom_call_target="tpu_custom_call" | custom-call | tf_op jit(solution)/shard_map/spread/pallas_call | solution.py:36
  2.1 10.5 %all-to-all-start = ((bf16[32,8,512]{2,1,0:T(8,128)(2,1)}), bf16[32,8,512]{2,1,0:T(8,128)(2,1)S(1)}, u32[]{:S(2)}, u32[]{:S(2)}) async-start(bf16[32,8,512]{2,1,0:T(8,128)(2,1)} %spread.1), calls=%async_computation | async-start | bytes 524288 | tf_op jit(solution)/shard_map/all_to_all | solution.py:305
  13.2 0.0 copy-start.1
  13.2 1.2 %copy-done.1 = bf16[1,128,4096]{2,1,0:T(8,128)(2,1)S(1)} copy-done((bf16[1,128,4096]{2,1,0:T(8,128)(2,1)S(1)}, bf16[1,128,4096]{2,1,0:T(8,128)(2,1)}, u32[]{:S(2)}) %copy-start.1) | copy-done | bytes 1048600
  14.5 0.0 copy-start.2
  14.5 1.2 %copy-done.2 = bf16[1,128,4096]{2,1,0:T(8,128)(2,1)S(1)} copy-done((bf16[1,128,4096]{2,1,0:T(8,128)(2,1)S(1)}, bf16[1,128,4096]{2,1,0:T(8,128)(2,1)}, u32[]{:S(2)}) %copy-start.2) | copy-done | bytes 1048600
  15.7 0.0 copy-start
  15.7 0.0 copy-start.3
  15.7 1.2 %delta.1 = (f32[32,128]{1,0:T(8,128)S(1)}, bf16[128,4096]{1,0:T(8,128)(2,1)S(1)}) custom-call(s32[1]{0:T(128)S(6)} %sub.7.live_ref, bf16[128,4096]{1,0:T(8,128)(2,1)S(1)} %bitcast.13, bf16[128,4096]{1,0:T(8,128)(2,1)S(1)} %bitcast.14), custom_call_target="tpu_custom_call" | custom-call | flops 1572864 | bytes 2097152 | tf_op jit(solution)/shard_map/delta/pallas_call | solution.py:65
  16.9 6.9 %all-to-all-done = bf16[32,8,512]{2,1,0:T(8,128)(2,1)S(1)} async-done(((bf16[32,8,512]{2,1,0:T(8,128)(2,1)}), bf16[32,8,512]{2,1,0:T(8,128)(2,1)S(1)}, u32[]{:S(2)}, u32[]{:S(2)}) %all-to-all-start) | async-done | bytes 262176 | tf_op jit(solution)/shard_map/all_to_all | solution.py:305
  23.8 0.0 copy-done
  23.8 0.0 copy-done.3
  23.8 1.9 %near.1 = (bf16[512,512]{1,0:T(8,128)(2,1)S(1)}, bf16[256,2048]{1,0:T(8,128)(2,1)S(1)}) custom-call(bf16[128,4096]{1,0:T(8,128)(2,1)S(1)} %bitcast.9, bf16[128,4096]{1,0:T(8,128)(2,1)S(1)} %get-tuple-element.13.g_ref, f32[32,128]{1,0:T(8,128)S(1)} %bitcast.15, f32[32,128]{1,0:T(8,128)S(1)} %get-tuple-element.14.delta_ref, bf16[256,512]{1,0:T(8,128)(2,1)S(1)} %bitcast.11), custom_call_target="tpu_custom_call" | custom-call | flops 536870912 | bytes 1048576 | tf_op jit(solution)/shard_map/near/pallas_call | solution.py:221
  25.7 4.3 %collective-permute-start = (bf16[512,512]{1,0:T(8,128)(2,1)S(1)}, bf16[512,512]{1,0:T(8,128)(2,1)S(1)}, u32[]{:S(2)}, u32[]{:S(2)}) collective-permute-start(bf16[512,512]{1,0:T(8,128)(2,1)S(1)} %get-tuple-element.15), channel_id=1, source_target_pairs={{0,1},{1,0},{2,3},{3,2},{4,5},{5,4},{6,7},{7,6},{8,9},{9,8},{10,11... | collective-permute-start | bytes 1572872 | tf_op jit(solution)/shard_map/ppermute | solution.py:322
  30.1 0.4 near_rows.1.near_ref
  30.5 1.1 %collective-permute-done.packet_ref = bf16[512,512]{1,0:T(8,128)(2,1)S(1)} collective-permute-done((bf16[512,512]{1,0:T(8,128)(2,1)S(1)}, bf16[512,512]{1,0:T(8,128)(2,1)S(1)}, u32[]{:S(2)}, u32[]{:S(2)}) %collective-permute-start) | collective-permute-done | bytes 524320 | tf_op jit(solution)/shard_map/ppermute | solution.py:322
  31.6 2.1 %far.1 = (bf16[128,2048]{1,0:T(8,128)(2,1)S(1)}, f32[256,512]{1,0:T(8,128)S(1)}, bf16[128,4096]{1,0:T(8,128)(2,1)}) custom-call(bf16[128,4096]{1,0:T(8,128)(2,1)S(1)} %bitcast.10, bf16[128,4096]{1,0:T(8,128)(2,1)S(1)} %get-tuple-element.13.g_ref, f32[32,128]{1,0:T(8,128)S(1)} %bitcast.16, f32[32,128]{1,0:T(8,128)S(1)} %get-tuple-element.14.delta_ref, ...), custom_call_target="tpu_custom_call" | custom-call | flops 671088640 | bytes 1048576 | tf_op jit(solution)/shard_map/far/pallas_call | solution.py:221
  33.7 0.1 fusion
  33.8 15.2 %all_to_all.15 = bf16[32,8,512]{2,1,0:T(8,128)(2,1)S(1)} all-to-all(bf16[32,8,512]{2,1,0:T(8,128)(2,1)S(1)} %fusion), channel_id=1, replica_groups=mesh['prompt'=32,'comp'=16] {'prompt'}, dimensions={0} | all-to-all | bytes 524288 | tf_op jit(solution)/shard_map/all_to_all | solution.py:337
  48.9 0.1 reduce_sum.12
  49.0 21.6 %all_to_all.16.parts_ref = bf16[16,8,512]{2,1,0:T(8,128)(2,1)S(1)} all-to-all(bf16[16,8,512]{2,1,0:T(8,128)(2,1)S(1)} %broadcast_in_dim.4), channel_id=1, replica_groups=mesh['prompt'=32,'comp'=16] {'comp'}, dimensions={0} | all-to-all | bytes 262144 | tf_op jit(solution)/shard_map/all_to_all | solution.py:339
  70.6 0.8 %finish.1 = (bf16[8,512]{1,0:T(8,128)(2,1)}, bf16[8,512]{1,0:T(8,128)(2,1)}, bf16[128,4096]{1,0:T(8,128)(2,1)}) custom-call(bf16[16,8,512]{2,1,0:T(8,128)(2,1)S(1)} %all_to_all.16.parts_ref, bf16[128,2048]{1,0:T(8,128)(2,1)S(1)} %get-tuple-element.18.far_ref, bf16[128,4096]{1,0:T(8,128)(2,1)} %get-tuple-element.19.before_hbm), custom_call_target="tpu_custom_call", output_to_operand_aliasing={{2}: (2, {})} | custom-call | tf_op jit(solution)/shard_map/finish/pallas_call | solution.py:271
  (1 shorter events, 0.0 us)
Async XLA Ops:
  2.1 21.7 %all-to-all-start = ((bf16[32,8,512]{2,1,0:T(8,128)(2,1)}), bf16[32,8,512]{2,1,0:T(8,128)(2,1)S(1)}, u32[]{:S(2)}, u32[]{:S(2)}) async-start(bf16[32,8,512]{2,1,0:T(8,128)(2,1)} %spread.1), calls=%async_computation | async-start | bytes 524288 | tf_op jit(solution)/shard_map/all_to_all | solution.py:305
  13.2 1.2 %copy-start.1 = (bf16[1,128,4096]{2,1,0:T(8,128)(2,1)S(1)}, bf16[1,128,4096]{2,1,0:T(8,128)(2,1)}, u32[]{:S(2)}) copy-start(bf16[1,128,4096]{2,1,0:T(8,128)(2,1)} %param.8) | copy-start | bytes 3145732
  14.5 1.2 %copy-start.2 = (bf16[1,128,4096]{2,1,0:T(8,128)(2,1)S(1)}, bf16[1,128,4096]{2,1,0:T(8,128)(2,1)}, u32[]{:S(2)}) copy-start(bf16[1,128,4096]{2,1,0:T(8,128)(2,1)} %param.9) | copy-start | bytes 3145732
  15.7 8.1 %copy-start = (bf16[1,128,4096]{2,1,0:T(8,128)(2,1)S(1)}, bf16[1,128,4096]{2,1,0:T(8,128)(2,1)}, u32[]{:S(2)}) copy-start(bf16[1,128,4096]{2,1,0:T(8,128)(2,1)} %param.7) | copy-start | bytes 3145732
  15.7 8.1 %copy-start.3 = (f32[1,32,128]{2,1,0:T(8,128)S(1)}, f32[1,32,128]{2,1,0:T(8,128)}, u32[]{:S(2)}) copy-start(f32[1,32,128]{2,1,0:T(8,128)} %param.10) | copy-start | bytes 49156
  25.7 5.9 %collective-permute-start = (bf16[512,512]{1,0:T(8,128)(2,1)S(1)}, bf16[512,512]{1,0:T(8,128)(2,1)S(1)}, u32[]{:S(2)}, u32[]{:S(2)}) collective-permute-start(bf16[512,512]{1,0:T(8,128)(2,1)S(1)} %get-tuple-element.15), channel_id=1, source_target_pairs={{0,1},{1,0},{2,3},{3,2},{4,5},{5,4},{6,7},{7,6},{8,9},{9,8},{10,11... | collective-permute-start | bytes 1572872 | tf_op jit(solution)/shard_map/ppermute | solution.py:322
